TPU v7x, 512 devices: a whole 4x8x8 slice. The times are simulated.
512 devices in a mesh: seq: 128 (over y, z, core), section: 4 (over x).
Axes of the slice: x: 4, y: 8, z: 8, core: 2. Of those that a mesh axis runs over, the one named last changes fastest.
Arguments:
- block_input: bfloat16 [4, 32768, 512], P('section', 'seq'), may hold values from -8 to 8
- upstream: bfloat16 [4, 32768, 512], P('section', 'seq'), may hold values from -6 to 6
- w_qkv: bfloat16 [4, 512, 768], P('section'), may hold values from -2 to 2
- w_out: bfloat16 [4, 256, 512], P('section'), may hold values from -0.375 to 0.375
- layer_norm_gain: float32 [4, 512], P('section'), may hold values from 0.1 to 1.9
- layer_norm_bias: float32 [4, 512], P('section'), may hold values from -3 to 3
- send_order: int32 [4, 128, 256], P('section', 'seq'), may hold values from 0 to 255, each once within a row
- recv_order: int32 [4, 128, 256], P('section', 'seq'), may hold values from 0 to 255, each once within a row
- patch_lengths: int32 [4, 128, 2], P('section', 'seq'), may hold values from 1 to 224, 256 in all within a row
Outputs:
- handed: bfloat16 [4, 32768, 512], P('section', 'seq')
Inputs may be any that keep to these rules, and one draw needn't show every extreme that they name: `send_order`: each device's row is a permutation of 0 to 255. `recv_order`: each device's row is a permutation of 0 to 255. `patch_lengths`: each device's lengths sum to 256; the largest is at most 224.
All inputs are finite; a program needn't handle non-finite values.
Results may differ from a plain program's by a relative error of at most 0.009.
The roundings to bfloat16 on the way count: a program that leaves them out, or rounds other values in their place, can miss the bound.
Values may be sent and summed in bfloat16 or wider, within the bound.
No kernel may reach another device: no remote copies, remote signals or barrier semaphores. Data moves between devices by JAX's collectives and lax.ppermute only.
A program may use at most 64 MiB of HBM per device.

v0:
```python
import jax
import jax.numpy as jnp
from jax import lax
from jax.sharding import PartitionSpec as P

HEAD = 16


def from_behind(array, axis, by):
    peers = lax.axis_size(axis)
    pairs = [(i, i + by) for i in range(peers) if 0 <= i + by < peers]
    return lax.ppermute(array, axis, pairs)


def layer_normalize(rows, gain_weight, shift_bias):
    values = rows.astype(jnp.float32)
    centered_rows = values - jnp.mean(values, axis=-1, keepdims=True)
    inverse_deviation = lax.rsqrt(
        jnp.mean(centered_rows * centered_rows, axis=-1, keepdims=True) + 1e-05
    )
    standardized_input = centered_rows * inverse_deviation
    normalized_rows = (standardized_input * gain_weight + shift_bias).astype(jnp.bfloat16)
    return (normalized_rows, standardized_input, inverse_deviation)


def layer_norm_backward(normed_gradient, standardized_input, inverse_deviation, gain_weight):
    incoming_gradient = normed_gradient * gain_weight
    gradient_mean = jnp.mean(incoming_gradient, axis=-1, keepdims=True)
    cross_term_mean = jnp.mean(incoming_gradient * standardized_input, axis=-1, keepdims=True)
    return inverse_deviation * (
        incoming_gradient - gradient_mean - standardized_input * cross_term_mean
    )


def attend_grad(qkv, out_grad, lengths):
    count = qkv.shape[0]
    width = out_grad.shape[1]
    heads = width // HEAD
    scale = float(HEAD) ** (-0.5)
    bounds = jnp.cumsum(lengths)
    places = jnp.arange(count, dtype=jnp.int32)
    segment = jnp.sum((places[:, None] >= bounds[None, :]).astype(jnp.int32), axis=1)
    same = segment[:, None] == segment[None, :]
    contract_last = (((1,), (1,)), ((), ()))
    contract_first = (((0,), (0,)), ((), ()))

    def one_head(head, grads):
        query = lax.dynamic_slice_in_dim(qkv, head * HEAD, HEAD, 1)
        key_part = lax.dynamic_slice_in_dim(qkv, width + head * HEAD, HEAD, 1)
        value = lax.dynamic_slice_in_dim(qkv, 2 * width + head * HEAD, HEAD, 1)
        dout = lax.dynamic_slice_in_dim(out_grad, head * HEAD, HEAD, 1)
        scores = (
            lax.dot_general(query, key_part, contract_last, preferred_element_type=jnp.float32)
            * scale
        )
        scores = jnp.where(same, scores, -1e30)
        top = jnp.max(scores, axis=-1, keepdims=True)
        expo = jnp.exp(scores - top)
        probs = expo / jnp.sum(expo, axis=-1, keepdims=True)
        weights = probs.astype(jnp.bfloat16)
        dprob = lax.dot_general(dout, value, contract_last, preferred_element_type=jnp.float32)
        inner = jnp.sum(dprob * probs, axis=-1, keepdims=True)
        dscore = (scale * probs * (dprob - inner)).astype(jnp.bfloat16)
        dquery = jnp.dot(dscore, key_part, preferred_element_type=jnp.float32).astype(jnp.bfloat16)
        dkey = lax.dot_general(
            dscore, query, contract_first, preferred_element_type=jnp.float32
        ).astype(jnp.bfloat16)
        dvalue = lax.dot_general(
            weights, dout, contract_first, preferred_element_type=jnp.float32
        ).astype(jnp.bfloat16)
        grads = lax.dynamic_update_slice_in_dim(grads, dquery, head * HEAD, 1)
        grads = lax.dynamic_update_slice_in_dim(grads, dkey, width + head * HEAD, 1)
        grads = lax.dynamic_update_slice_in_dim(grads, dvalue, 2 * width + head * HEAD, 1)
        return grads

    empty = jnp.zeros((count, 3 * width), jnp.bfloat16)
    return lax.fori_loop(0, heads, one_head, empty)


def per_device(
    block_input,
    upstream,
    w_qkv,
    w_out,
    layer_norm_gain,
    layer_norm_bias,
    send_order,
    recv_order,
    patch_lengths,
):
    inputs = block_input[0]
    upper = upstream[0]
    projection = w_qkv[0]
    gain_weight = layer_norm_gain[0]
    shift_bias = layer_norm_bias[0]
    sending = send_order[0, 0]
    placing = recv_order[0, 0]
    lengths = patch_lengths[0, 0]
    undo_send = jnp.argsort(sending)
    undo_place = jnp.argsort(placing)
    contract_last = (((1,), (1,)), ((), ()))
    out_common = lax.dot_general(
        upper, w_out[0], contract_last, preferred_element_type=jnp.float32
    ).astype(jnp.bfloat16)
    out_sent = out_common[sending]
    patch_token_rows = lax.all_to_all(
        inputs[sending], "seq", split_axis=0, concat_axis=0, tiled=True
    )[placing]
    normalized_rows, standardized_input, inverse_deviation = layer_normalize(
        patch_token_rows, gain_weight, shift_bias
    )
    qkv = jnp.dot(normalized_rows, projection, preferred_element_type=jnp.float32).astype(
        jnp.bfloat16
    )
    out_grad = lax.all_to_all(out_sent, "seq", split_axis=0, concat_axis=0, tiled=True)[placing]
    dqkv = attend_grad(qkv, out_grad, lengths)
    normed_gradient = lax.dot_general(
        dqkv, projection, contract_last, preferred_element_type=jnp.float32
    )
    patch_attention_branch = layer_norm_backward(
        normed_gradient, standardized_input, inverse_deviation, gain_weight
    ).astype(jnp.bfloat16)
    branch_output = lax.all_to_all(
        patch_attention_branch[undo_place], "seq", split_axis=0, concat_axis=0, tiled=True
    )[undo_send]
    total = (upper.astype(jnp.float32) + branch_output.astype(jnp.float32)).astype(jnp.bfloat16)
    handed = from_behind(total, "section", -1)
    return handed[None]


def solution(mesh):
    return jax.shard_map(
        per_device,
        mesh=mesh,
        in_specs=(
            P("section", "seq", None),
            P("section", "seq", None),
            P("section", None, None),
            P("section", None, None),
            P("section", None),
            P("section", None),
            P("section", "seq", None),
            P("section", "seq", None),
            P("section", "seq", None),
        ),
        out_specs=P("section", "seq", None),
        check_vma=False,
    )
```

profile of v0, /device:TPU:1, one launch (start us, length us, event | category | flops | bytes accessed | tf_op | source)
XLA Modules:
  0.0 118.7 jit_solution(1688347295094257577)
XLA Ops:
  0.0 0.8 compare_select_fusion.1
  0.8 1.3 %convolution_convert_fusion.4 = bf16[256,256]{1,0:T(8,128)(2,1)S(1)} fusion(bf16[1,256,512]{2,1,0:T(8,128)(2,1)} %param.14, bf16[1,256,512]{2,1,0:T(8,128)(2,1)} %param.12), kind=kOutput, calls=%fused_computation.36 | convolution fusion | flops 67174400 | bytes 655360 | tf_op jit(solution)/shard_map/dot_general | solution.py:102
  2.1 1.2 gather_fusion.2
  3.2 0.7 all_to_all.27
  3.9 18.4 %all-to-all-start.1 = ((bf16[128,2,256]{2,1,0:T(2,128)(2,1)}), bf16[128,2,256]{2,1,0:T(2,128)(2,1)S(1)}, u32[]{:S(2)}, u32[]{:S(2)}) async-start(bf16[128,2,256]{2,1,0:T(2,128)(2,1)} %all_to_all.27), calls=%async_computation.1 | async-start | bytes 262144 | tf_op jit(solution)/shard_map/all_to_all | solution.py:115
  22.3 1.2 gather_fusion
  23.5 0.8 all_to_all.24
  24.3 0.7 copy-done.7
  25.1 0.7 copy-done.3
  25.8 3.2 %sort.31 = (s32[256]{0:T(256)}, s32[256]{0:T(256)S(1)}) sort(s32[256]{0:T(256)S(1)} %bitcast.39, s32[256]{0:T(256)S(1)} %iota.11), dimensions={0}, to_apply=%region_11.12 | sort | flops 2048 | bytes 4096 | tf_op jit(solution)/shard_map/jit(argsort)/sort | solution.py:100
  29.0 5.5 %all-to-all-done.1 = bf16[128,2,256]{2,1,0:T(2,128)(2,1)S(1)} async-done(((bf16[128,2,256]{2,1,0:T(2,128)(2,1)}), bf16[128,2,256]{2,1,0:T(2,128)(2,1)S(1)}, u32[]{:S(2)}, u32[]{:S(2)}) %all-to-all-start.1) | async-done | bytes 131104 | tf_op jit(solution)/shard_map/all_to_all | solution.py:115
  34.5 8.2 %all-to-all-start = ((bf16[128,2,512]{2,1,0:T(2,128)(2,1)}), bf16[128,2,512]{2,1,0:T(2,128)(2,1)S(1)}, u32[]{:S(2)}, u32[]{:S(2)}) async-start(bf16[128,2,512]{2,1,0:T(2,128)(2,1)} %all_to_all.24), calls=%async_computation | async-start | bytes 524288 | tf_op jit(solution)/shard_map/all_to_all | solution.py:106
  42.9 1.2 gather_fusion.3
  44.1 12.9 %all-to-all-done = bf16[128,2,512]{2,1,0:T(2,128)(2,1)S(1)} async-done(((bf16[128,2,512]{2,1,0:T(2,128)(2,1)}), bf16[128,2,512]{2,1,0:T(2,128)(2,1)S(1)}, u32[]{:S(2)}, u32[]{:S(2)}) %all-to-all-start) | async-done | bytes 262176 | tf_op jit(solution)/shard_map/all_to_all | solution.py:106
  57.1 1.2 gather_fusion.1
  58.6 0.4 copy-done.6
  59.3 0.4 convolution_convert_fusion.3
  59.8 24.9 %while.16 = (s32[]{:T(128)}, bf16[256,768]{0,1:T(8,128)(2,1)S(1)}, bf16[256,768]{1,0:T(8,128)(2,1)S(1)}, bf16[256,256]{1,0:T(8,128)(2,1)S(1)}, s32[256]{0:T(256)...) while((s32[]{:T(128)}, bf16[256,768]{0,1:T(8,128)(2,1)S(1)}, ...), condition=%wide.region_8.9_spmd.clone, body=%wide.region_4.0_spmd.clone.sunk | while | flops 11742479 | bytes 2725180 | solution.py:77
  64.4 0.3 fusion.67
  69.1 0.3 fusion.67
  75.3 0.3 fusion.67
  84.7 0.6 fusion.45
  85.4 1.2 gather_fusion.4
  86.6 0.8 all_to_all.30
  87.4 7.0 %all-to-all-start.2 = ((bf16[128,2,512]{2,1,0:T(2,128)(2,1)}), bf16[128,2,512]{2,1,0:T(2,128)(2,1)S(1)}, u32[]{:S(2)}, u32[]{:S(2)}) async-start(bf16[128,2,512]{2,1,0:T(2,128)(2,1)} %all_to_all.30), calls=%async_computation.2 | async-start | bytes 524288 | tf_op jit(solution)/shard_map/all_to_all | solution.py:123
  94.4 0.7 copy-done.4
  95.1 3.2 %sort.32 = (s32[256]{0:T(256)}, s32[256]{0:T(256)S(1)}) sort(s32[256]{0:T(256)S(1)} %bitcast.40, s32[256]{0:T(256)S(1)} %iota.12), dimensions={0}, to_apply=%region_12.13 | sort | flops 2048 | bytes 4096 | tf_op jit(solution)/shard_map/jit(argsort)/sort | solution.py:99
  98.3 10.4 %all-to-all-done.2 = bf16[128,2,512]{2,1,0:T(2,128)(2,1)S(1)} async-done(((bf16[128,2,512]{2,1,0:T(2,128)(2,1)}), bf16[128,2,512]{2,1,0:T(2,128)(2,1)S(1)}, u32[]{:S(2)}, u32[]{:S(2)}) %all-to-all-start.2) | async-done | bytes 262176 | tf_op jit(solution)/shard_map/all_to_all | solution.py:123
  108.9 1.2 gather_fusion.5
  110.1 1.3 %collective-permute-start = (bf16[256,512]{1,0:T(8,128)(2,1)S(1)}, bf16[256,512]{1,0:T(8,128)(2,1)S(1)}, u32[]{:S(2)}, u32[]{:S(2)}) collective-permute-start(bf16[256,512]{1,0:T(8,128)(2,1)S(1)} %add_convert_fusion), channel_id=1, source_target_pairs={{1,0},{2,1},{3,2},{5,4},{6,5},{7,6},{9,8},{10,9},{11,10},{13,12},{... | collective-permute-start | bytes 786440 | tf_op jit(solution)/shard_map/ppermute | solution.py:12
  111.4 6.6 %collective-permute-done = bf16[256,512]{1,0:T(8,128)(2,1)S(1)} collective-permute-done((bf16[256,512]{1,0:T(8,128)(2,1)S(1)}, bf16[256,512]{1,0:T(8,128)(2,1)S(1)}, u32[]{:S(2)}, u32[]{:S(2)}) %collective-permute-start) | collective-permute-done | bytes 262176 | tf_op jit(solution)/shard_map/ppermute | solution.py:12
  118.0 0.7 copy.20
  (143 shorter events, 25.1 us)
Async XLA Ops:
  0.0 58.6 %copy-start = (bf16[1,512,768]{2,1,0:T(8,128)(2,1)S(1)}, bf16[1,512,768]{2,1,0:T(8,128)(2,1)}, u32[]{:S(2)}) copy-start(bf16[1,512,768]{2,1,0:T(8,128)(2,1)} %param.13) | copy-start | bytes 2359300
  3.2 19.1 %copy-start.1 = (bf16[1,256,512]{2,1,0:T(8,128)(2,1)S(1)}, bf16[1,256,512]{2,1,0:T(8,128)(2,1)}, u32[]{:S(2)}) copy-start(bf16[1,256,512]{2,1,0:T(8,128)(2,1)} %param.11) | copy-start | bytes 786436
  3.9 30.6 %all-to-all-start.1 = ((bf16[128,2,256]{2,1,0:T(2,128)(2,1)}), bf16[128,2,256]{2,1,0:T(2,128)(2,1)S(1)}, u32[]{:S(2)}, u32[]{:S(2)}) async-start(bf16[128,2,256]{2,1,0:T(2,128)(2,1)} %all_to_all.27), calls=%async_computation.1 | async-start | bytes 262144 | tf_op jit(solution)/shard_map/all_to_all | solution.py:115
  24.3 0.7 copy-start.7
  25.1 0.7 copy-start.3
  34.5 22.4 %all-to-all-start = ((bf16[128,2,512]{2,1,0:T(2,128)(2,1)}), bf16[128,2,512]{2,1,0:T(2,128)(2,1)S(1)}, u32[]{:S(2)}, u32[]{:S(2)}) async-start(bf16[128,2,512]{2,1,0:T(2,128)(2,1)} %all_to_all.24), calls=%async_computation | async-start | bytes 524288 | tf_op jit(solution)/shard_map/all_to_all | solution.py:106
  58.4 0.7 copy-start.6
  58.6 0.7 copy-start.5
  87.4 21.3 %all-to-all-start.2 = ((bf16[128,2,512]{2,1,0:T(2,128)(2,1)}), bf16[128,2,512]{2,1,0:T(2,128)(2,1)S(1)}, u32[]{:S(2)}, u32[]{:S(2)}) async-start(bf16[128,2,512]{2,1,0:T(2,128)(2,1)} %all_to_all.30), calls=%async_computation.2 | async-start | bytes 524288 | tf_op jit(solution)/shard_map/all_to_all | solution.py:123
  94.4 0.7 copy-start.4
  108.8 1.2 copy-start.2
  110.1 7.9 %collective-permute-start = (bf16[256,512]{1,0:T(8,128)(2,1)S(1)}, bf16[256,512]{1,0:T(8,128)(2,1)S(1)}, u32[]{:S(2)}, u32[]{:S(2)}) collective-permute-start(bf16[256,512]{1,0:T(8,128)(2,1)S(1)} %add_convert_fusion), channel_id=1, source_target_pairs={{1,0},{2,1},{3,2},{5,4},{6,5},{7,6},{9,8},{10,9},{11,10},{13,12},{... | collective-permute-start | bytes 786440 | tf_op jit(solution)/shard_map/ppermute | solution.py:12
where the time goes:
time: 120 us; the launch traced here: 119 us
  waiting for transfers between devices  35.5 us (30%)
  starting transfers between devices  34.9 us (29%)
  matrix products  24.5 us (20%)
  local copies, waits for them, and re-layouts  12.9 us (11%)
  other arithmetic  10.4 us (9%)
    all_to_all x1, starting transfers between devices, per_device(): lax.all_to_all(out_sent, 'seq', split_axis=0, concat_axis=0, tiled=True)  18.4 us
    all_to_all x1, waiting for transfers between devices, per_device(): lax.all_to_all(inputs[sending], 'seq', split_axis=0, concat_axis=0, tiled...  12.9 us
    all_to_all x1, waiting for transfers between devices, per_device(): lax.all_to_all(patch_attention_branch[undo_place], 'seq', split_axis=0, c...  10.4 us
    all_to_all x1, starting transfers between devices, per_device(): lax.all_to_all(inputs[sending], 'seq', split_axis=0, concat_axis=0, tiled...  8.19 us
    all_to_all x1, starting transfers between devices, per_device(): lax.all_to_all(patch_attention_branch[undo_place], 'seq', split_axis=0, c...  6.97 us
    ppermute x1, waiting for transfers between devices, from_behind(): return lax.ppermute(array, axis, pairs)  6.64 us
    all_to_all x1, waiting for transfers between devices, per_device(): lax.all_to_all(out_sent, 'seq', split_axis=0, concat_axis=0, tiled=True)  5.54 us
    dot_general x16, matrix products, one_head(): lax.dot_general(query, key_part, contract_last, preferred_element_type=jn...  5.11 us
  transfers between devices with their start and end apart: 4, of which 4 were waited for; matrix products, arithmetic and copies ran while one was open for 8% of the time, Pallas kernels for 0%

commit v1 on v0

v1 whole, which is shorter than its diff:
```python
import jax
import jax.numpy as jnp
from jax import lax
from jax.experimental import pallas as pl
from jax.experimental.pallas import tpu as pltpu
from jax.sharding import PartitionSpec as P

HEAD = 16
GROUP = 128 // HEAD
MASKED = -(2.0**99)
BF = jnp.bfloat16
F32 = jnp.float32
ROWS_BY_ROWS = (((0,), (0,)), ((), ()))
LAST_BY_LAST = (((1,), (1,)), ((), ()))
ROWS_BY_LAST = (((0,), (1,)), ((), ()))


def dot(a, b, dims=(((1,), (0,)), ((), ()))):
    return lax.dot_general(a, b, dims, preferred_element_type=F32)


def selection(order):
    count = order.shape[1]
    wanted = lax.broadcasted_iota(jnp.int32, (count, count), 0)
    return jnp.where(wanted == order, 1.0, 0.0).astype(BF)


def pre_kernel(rows_ref, upper_ref, w_out_ref, order_ref, sent_ref):
    pick = selection(order_ref[...])
    out_common = dot(upper_ref[0], w_out_ref[0], LAST_BY_LAST).astype(BF)
    both = jnp.concatenate([rows_ref[0], out_common], axis=1)
    sent_ref[...] = dot(pick, both, ROWS_BY_ROWS).astype(BF).reshape(sent_ref.shape)


def main_kernel(got_ref, order_ref, lengths_ref, w_ref, gain_ref, shift_ref, sent_ref, grads_ref):
    count = order_ref.shape[1]
    projection = w_ref[0]
    model = projection.shape[0]
    width = projection.shape[1] // 3
    gain = gain_ref[...]
    place = selection(order_ref[...])
    got = dot(place, got_ref[...].reshape(count, model + width), ROWS_BY_ROWS)

    values = got[:, :model]
    centered = values - jnp.mean(values, axis=-1, keepdims=True)
    inverse = lax.rsqrt(jnp.mean(centered * centered, axis=-1, keepdims=True) + 1e-05)
    standardized = centered * inverse
    normed = (standardized * gain + shift_ref[...]).astype(BF)
    qkv = dot(normed, projection).astype(BF)
    dout = got[:, model:].astype(BF)

    scale = float(HEAD) ** (-0.5)
    query_t = (qkv[:, :width] * scale).T
    key_part = qkv[:, width : 2 * width]
    key_t = (key_part * scale).T
    value = qkv[:, 2 * width :]
    dout_t = dout.T

    first = lengths_ref[0, 0]
    key_at = (lax.broadcasted_iota(jnp.int32, (count, 128), 0) < first).astype(jnp.int32)
    lane = lax.broadcasted_iota(jnp.int32, (count, 128), 1)
    key_mark = jnp.where(lane == key_at, 1.0, 0.0).astype(BF)
    query_at = (lax.broadcasted_iota(jnp.int32, (128, count), 1) >= first).astype(jnp.int32)
    sub = lax.broadcasted_iota(jnp.int32, (128, count), 0)
    query_mark = jnp.where(sub == query_at, MASKED, 0.0).astype(BF)

    for head in range(width // HEAD):
        group, at = divmod(head, GROUP)
        lanes = slice(group * 128, group * 128 + 128)
        mine = slice(head * HEAD, head * HEAD + HEAD)

        def padded(block):
            parts = [block]
            if at > 0:
                parts.insert(0, jnp.zeros((at * HEAD, count), BF))
            if at < GROUP - 1:
                parts.append(jnp.zeros(((GROUP - 1 - at) * HEAD, count), BF))
            return jnp.concatenate(parts, axis=0)

        scores = dot(
            jnp.concatenate([key_part[:, lanes], key_mark], axis=1),
            jnp.concatenate([padded(query_t[mine]), query_mark], axis=0),
        )
        top = jnp.max(scores, axis=0, keepdims=True)
        expo = jnp.exp(scores - top)
        probs = expo * (1.0 / jnp.sum(expo, axis=0, keepdims=True))
        dprob = dot(value[:, lanes], padded(dout_t[mine]))
        inner = jnp.sum(dprob * probs, axis=0, keepdims=True)
        dscore = (probs * (dprob - inner)).astype(BF)
        grads_ref[mine] = dot(key_t[mine], dscore).astype(BF)
        grads_ref[slice(width + mine.start, width + mine.stop)] = dot(
            query_t[mine], dscore, LAST_BY_LAST
        ).astype(BF)
        grads_ref[slice(2 * width + mine.start, 2 * width + mine.stop)] = dot(
            dout_t[mine], probs.astype(BF), LAST_BY_LAST
        ).astype(BF)

    incoming = dot(grads_ref[...], projection, ROWS_BY_LAST) * gain
    mean = jnp.mean(incoming, axis=-1, keepdims=True)
    cross = jnp.mean(incoming * standardized, axis=-1, keepdims=True)
    branch = (inverse * (incoming - mean - standardized * cross)).astype(BF)
    sent_ref[...] = dot(place, branch).astype(BF).reshape(sent_ref.shape)


def post_kernel(got_ref, upper_ref, order_ref, total_ref):
    count, model = total_ref.shape
    branch = dot(selection(order_ref[...]), got_ref[...].reshape(count, model))
    total_ref[...] = (upper_ref[0].astype(F32) + branch).astype(BF)


def regroup(array):
    return lax.all_to_all(array, "seq", split_axis=0, concat_axis=0, tiled=True)


def per_device(
    block_input,
    upstream,
    w_qkv,
    w_out,
    layer_norm_gain,
    layer_norm_bias,
    send_order,
    recv_order,
    patch_lengths,
):
    _, count, model = block_input.shape
    width = w_out.shape[1]
    peers = lax.axis_size("seq")
    each = count // peers
    sending, placing, lengths = send_order[0], recv_order[0], patch_lengths[0]

    sent = pl.pallas_call(
        pre_kernel,
        out_shape=jax.ShapeDtypeStruct((peers, each, model + width), BF),
    )(block_input, upstream, w_out, sending)
    got = regroup(sent)
    vmem = pl.BlockSpec(memory_space=pltpu.VMEM)
    back = pl.pallas_call(
        main_kernel,
        out_shape=jax.ShapeDtypeStruct((peers, each, model), BF),
        in_specs=[vmem, vmem, pl.BlockSpec(memory_space=pltpu.SMEM), vmem, vmem, vmem],
        out_specs=vmem,
        scratch_shapes=[pltpu.VMEM((3 * width, count), BF)],
        compiler_params=pltpu.CompilerParams(vmem_limit_bytes=32 * 1024 * 1024),
    )(got, placing, lengths, w_qkv, layer_norm_gain, layer_norm_bias)
    back = regroup(back)
    total = pl.pallas_call(
        post_kernel,
        out_shape=jax.ShapeDtypeStruct((count, model), BF),
    )(back, upstream, sending)
    sections = lax.axis_size("section")
    handed = lax.ppermute(total, "section", [(s, s - 1) for s in range(1, sections)])
    return handed[None]


def solution(mesh):
    return jax.shard_map(
        per_device,
        mesh=mesh,
        in_specs=(
            P("section", "seq", None),
            P("section", "seq", None),
            P("section", None, None),
            P("section", None, None),
            P("section", None),
            P("section", None),
            P("section", "seq", None),
            P("section", "seq", None),
            P("section", "seq", None),
        ),
        out_specs=P("section", "seq", None),
        check_vma=False,
    )
```

time: 120 us -> 81.3 us (0.68)
  blocking collectives: 0 us -> 57 us
  starting transfers between devices: 34.9 us -> 1.28 us
  waiting for transfers between devices: 35.5 us -> 6.98 us
  matrix products: 24.5 us -> 0 us
  Pallas kernels: 0 us -> 13.3 us
  local copies, waits for them, and re-layouts: 12.9 us -> 1.39 us
  other arithmetic: 10.4 us -> 0 us
    all_to_all x0 -> x2, blocking collectives: none -> 57 us  [regroup(): return lax.all_to_all(array, 'seq', split_axis=0, concat_axis=0, tiled=True)]
    all_to_all x3 -> x0, starting transfers between devices: 33.6 us -> none  [the longest x1 18.4 us: per_device(): lax.all_to_all(out_sent, 'seq', split_axis=0, concat_axis=0, tiled=True)]
    all_to_all x3 -> x0, waiting for transfers between devices: 28.9 us -> none  [the longest x1 12.9 us: per_device(): lax.all_to_all(inputs[sending], 'seq', split_axis=0, concat_axis=0, tiled...]
    dot_general x83 -> x0, matrix products: 24.5 us -> none  [the longest x16 5.11 us: one_head(): lax.dot_general(query, key_part, contract_last, preferred_element_type=jn...]
    pallas_call x0 -> x3, Pallas kernels: none -> 13.3 us  [the longest x1 8.87 us: per_device(): pl.pallas_call(main_kernel, out_shape=jax.ShapeDtypeStruct((peers, each,...]
    gather x6 -> x0, local copies, waits for them, and re-layouts: 6.92 us -> none  [the longest x1 1.15 us: per_device(): inputs[sending]]
    sort x2 -> x0, other arithmetic: 6.37 us -> none  [the longest x1 3.19 us: per_device(): undo_send = jnp.argsort(sending)]
    all_to_all x6 -> x0, local copies, waits for them, and re-layouts: 2.57 us -> none  [the longest x2 0.91 us: per_device(): lax.all_to_all(inputs[sending], 'seq', split_axis=0, concat_axis=0, tiled...]
  transfers between devices with their start and end apart: 4 -> 1, of which waited for: 4 -> 1; matrix products, arithmetic and copies ran while one was open for 8% -> 0% of each run, Pallas kernels for 0% -> 0%
where the time goes in v1:
time: 81.3 us; the launch traced here: 80 us
  blocking collectives  57 us (70%)
  Pallas kernels  13.3 us (16%)
  waiting for transfers between devices  6.98 us (9%)
  local copies, waits for them, and re-layouts  1.39 us (2%)
  starting transfers between devices  1.28 us (2%)
    all_to_all x2, blocking collectives, regroup(): return lax.all_to_all(array, 'seq', split_axis=0, concat_axis=0, tiled=True)  57 us
    pallas_call x1, Pallas kernels, per_device(): pl.pallas_call(main_kernel, out_shape=jax.ShapeDtypeStruct((peers, each,...  8.87 us
    ppermute x1, waiting for transfers between devices, per_device(): lax.ppermute(total, 'section', [(s, s - 1) for s in range(1, sections)])  6.98 us
    pallas_call x1, Pallas kernels, per_device(): pl.pallas_call(pre_kernel, out_shape=jax.ShapeDtypeStruct((peers, each, m...  2.45 us
    pallas_call x1, Pallas kernels, per_device(): pl.pallas_call(post_kernel, out_shape=jax.ShapeDtypeStruct((count, model)...  1.97 us
  transfers between devices with their start and end apart: 1, of which 1 were waited for; matrix products, arithmetic and copies ran while one was open for 0% of the time, Pallas kernels for 0%

profile of v1, /device:TPU:1, one launch (start us, length us, event | category | flops | bytes accessed | tf_op | source)
XLA Modules:
  0.0 80.0 jit_solution(10945008966439736514)
XLA Ops:
  0.0 0.0 copy-start
  0.0 2.4 %shard_map.91 = bf16[128,2,768]{2,1,0:T(2,128)(2,1)} custom-call(bf16[1,256,512]{2,1,0:T(8,128)(2,1)} %rows_ref.1, bf16[1,256,512]{2,1,0:T(8,128)(2,1)} %upper_ref.3, bf16[1,256,512]{2,1,0:T(8,128)(2,1)} %w_out_ref.1, s32[1,256]{1,0:T(1,128)} %bitcast.7), custom_call_target="tpu_custom_call" | custom-call | tf_op jit(solution)/shard_map/pallas_call | solution.py:132
  2.4 0.0 copy-start.2
  2.5 35.4 %all_to_all.10.got_ref = bf16[128,2,768]{2,1,0:T(2,128)(2,1)S(1)} all-to-all(bf16[128,2,768]{2,1,0:T(2,128)(2,1)} %shard_map.91), channel_id=1, replica_groups=mesh['seq'=128,'section'=4] {'seq'}, dimensions={0} | all-to-all | bytes 786432 | tf_op jit(solution)/shard_map/all_to_all | solution.py:112
  37.8 0.0 copy-start.1
  37.8 0.0 copy-start.3
  37.8 0.0 copy-start.4
  37.8 0.0 copy-done
  37.8 0.0 copy-done.2
  37.8 0.7 copy-done.1
  38.5 0.0 copy-done.3
  38.5 0.0 copy-done.4
  38.5 8.9 %shard_map.92 = bf16[128,2,512]{2,1,0:T(2,128)(2,1)S(1)} custom-call(bf16[128,2,768]{2,1,0:T(2,128)(2,1)S(1)} %all_to_all.10.got_ref, s32[1,256]{1,0:T(1,128)S(1)} %bitcast.4, s32[1,2]{1,0:T(1,128)S(1)} %bitcast.5, bf16[1,512,768]{2,1,0:T(8,128)(2,1)S(1)} %copy-done, f32[1,512]{1,0:T(1,128)S(1)} %copy-done.1, f32[1,512]{1,0:T(1,128)S(1)} %copy-done.2), custom_call_target="tpu_custom_call" | custom-call | tf_op jit(solution)/shard_map/pallas_call | solution.py:138
  47.4 21.7 %all_to_all.11.got_ref = bf16[128,2,512]{2,1,0:T(2,128)(2,1)} all-to-all(bf16[128,2,512]{2,1,0:T(2,128)(2,1)S(1)} %shard_map.92), channel_id=1, replica_groups=mesh['seq'=128,'section'=4] {'seq'}, dimensions={0} | all-to-all | bytes 524288 | tf_op jit(solution)/shard_map/all_to_all | solution.py:112
  69.0 2.0 %shard_map.93 = bf16[256,512]{1,0:T(8,128)(2,1)} custom-call(bf16[128,2,512]{2,1,0:T(2,128)(2,1)} %all_to_all.11.got_ref, bf16[1,256,512]{2,1,0:T(8,128)(2,1)} %upper_ref.3, s32[1,256]{1,0:T(1,128)} %bitcast.8), custom_call_target="tpu_custom_call" | custom-call | tf_op jit(solution)/shard_map/pallas_call | solution.py:147
  71.0 1.3 %collective-permute-start = (bf16[256,512]{1,0:T(8,128)(2,1)}, bf16[256,512]{1,0:T(8,128)(2,1)S(1)}, u32[]{:S(2)}, u32[]{:S(2)}) collective-permute-start(bf16[256,512]{1,0:T(8,128)(2,1)} %shard_map.93), channel_id=1, source_target_pairs={{1,0},{2,1},{3,2},{5,4},{6,5},{7,6},{9,8},{10,9},{11,10},{13,12},{... | collective-permute-start | bytes 786440 | tf_op jit(solution)/shard_map/ppermute | solution.py:152
  72.3 7.0 %collective-permute-done = bf16[256,512]{1,0:T(8,128)(2,1)S(1)} collective-permute-done((bf16[256,512]{1,0:T(8,128)(2,1)}, bf16[256,512]{1,0:T(8,128)(2,1)S(1)}, u32[]{:S(2)}, u32[]{:S(2)}) %collective-permute-start) | collective-permute-done | bytes 262176 | tf_op jit(solution)/shard_map/ppermute | solution.py:152
  79.3 0.7 copy.11
Async XLA Ops:
  0.0 37.8 %copy-start = (bf16[1,512,768]{2,1,0:T(8,128)(2,1)S(1)}, bf16[1,512,768]{2,1,0:T(8,128)(2,1)}, u32[]{:S(2)}) copy-start(bf16[1,512,768]{2,1,0:T(8,128)(2,1)} %w_ref.1) | copy-start | bytes 2359300
  2.4 35.4 %copy-start.2 = (f32[1,512]{1,0:T(1,128)S(1)}, f32[1,512]{1,0:T(1,128)}, u32[]{:S(2)}) copy-start(f32[1,512]{1,0:T(1,128)} %shift_ref.1) | copy-start | bytes 6148
  37.8 0.7 copy-start.1
  37.8 0.7 copy-start.3
  37.8 0.7 copy-start.4
  71.0 8.3 %collective-permute-start = (bf16[256,512]{1,0:T(8,128)(2,1)}, bf16[256,512]{1,0:T(8,128)(2,1)S(1)}, u32[]{:S(2)}, u32[]{:S(2)}) collective-permute-start(bf16[256,512]{1,0:T(8,128)(2,1)} %shard_map.93), channel_id=1, source_target_pairs={{1,0},{2,1},{3,2},{5,4},{6,5},{7,6},{9,8},{10,9},{11,10},{13,12},{... | collective-permute-start | bytes 786440 | tf_op jit(solution)/shard_map/ppermute | solution.py:152

commit v2 on v1

v2 whole, which is shorter than its diff:
```python
import jax
import jax.numpy as jnp
from jax import lax
from jax.experimental import pallas as pl
from jax.experimental.pallas import tpu as pltpu
from jax.sharding import PartitionSpec as P

HEAD = 16
GROUP = 128 // HEAD
MASKED = -(2.0**99)
BF = jnp.bfloat16
F32 = jnp.float32
ROWS_BY_ROWS = (((0,), (0,)), ((), ()))
LAST_BY_LAST = (((1,), (1,)), ((), ()))
ROWS_BY_LAST = (((0,), (1,)), ((), ()))


def dot(a, b, dims=(((1,), (0,)), ((), ()))):
    return lax.dot_general(a, b, dims, preferred_element_type=F32)


def selection(order):
    count = order.shape[1]
    wanted = lax.broadcasted_iota(jnp.int32, (count, count), 0)
    return jnp.where(wanted == order, 1.0, 0.0).astype(BF)


def pre_kernel(
    rows_hbm, upper_hbm, w_out_hbm, order_hbm, sent_ref, rows_ref, upper_ref, w_out_ref, order_ref, arrived
):
    pairs = [
        (order_hbm, order_ref),
        (upper_hbm.at[0], upper_ref),
        (w_out_hbm.at[0], w_out_ref),
        (rows_hbm.at[0], rows_ref),
    ]
    copies = [pltpu.make_async_copy(a, b, arrived.at[i]) for i, (a, b) in enumerate(pairs)]
    for copy in copies:
        copy.start()
    copies[0].wait()
    pick = selection(order_ref[...])
    copies[1].wait()
    copies[2].wait()
    out_common = dot(upper_ref[...], w_out_ref[...], LAST_BY_LAST).astype(BF)
    copies[3].wait()
    both = jnp.concatenate([rows_ref[...], out_common], axis=1)
    sent_ref[...] = dot(pick, both, ROWS_BY_ROWS).astype(BF).reshape(sent_ref.shape)


def prepare_kernel(
    upper_in,
    sending_in,
    placing_in,
    lengths_in,
    gain_in,
    shift_in,
    upper_ref,
    pick_ref,
    place_ref,
    key_mark_ref,
    query_mark_ref,
    gain_ref,
    shift_ref,
):
    upper_ref[...] = upper_in[0]
    pick_ref[...] = selection(sending_in[...])
    place_ref[...] = selection(placing_in[...])
    gain_ref[...] = gain_in[...]
    shift_ref[...] = shift_in[...]
    first = lengths_in[:, :1]
    count = placing_in.shape[1]
    key_at = (lax.broadcasted_iota(jnp.int32, (count, 128), 0) < first).astype(jnp.int32)
    lane = lax.broadcasted_iota(jnp.int32, (count, 128), 1)
    key_mark_ref[...] = jnp.where(lane == key_at, 1.0, 0.0).astype(BF)
    query_at = (lax.broadcasted_iota(jnp.int32, (128, count), 1) >= first).astype(jnp.int32)
    sub = lax.broadcasted_iota(jnp.int32, (128, count), 0)
    query_mark_ref[...] = jnp.where(sub == query_at, MASKED, 0.0).astype(BF)


def main_kernel(
    got_ref,
    place_ref,
    key_mark_ref,
    query_mark_ref,
    w_ref,
    gain_ref,
    shift_ref,
    sent_ref,
    dscore_ref,
    weights_ref,
    query_ref,
    dout_ref,
    dquery_ref,
    dothers_ref,
):
    count = place_ref.shape[0]
    projection = w_ref[0]
    model = projection.shape[0]
    width = projection.shape[1] // 3
    gain = gain_ref[...]
    place = place_ref[...]
    got = dot(place, got_ref[...].reshape(count, model + width), ROWS_BY_ROWS)

    values = got[:, :model]
    centered = values - jnp.mean(values, axis=-1, keepdims=True)
    inverse = lax.rsqrt(jnp.mean(centered * centered, axis=-1, keepdims=True) + 1e-05)
    standardized = centered * inverse
    normed = (standardized * gain + shift_ref[...]).astype(BF)
    qkv = dot(normed, projection).astype(BF)
    dout = got[:, model:].astype(BF)

    scale = float(HEAD) ** (-0.5)
    query = qkv[:, :width] * scale
    key_part = qkv[:, width : 2 * width]
    value = qkv[:, 2 * width :]
    query_t = query.T
    key_t = (key_part * scale).T
    dout_t = dout.T

    key_mark = key_mark_ref[...]
    query_mark = query_mark_ref[...]
    head_of = lax.broadcasted_iota(jnp.int32, (count, 128), 1) // HEAD

    for head in range(width // HEAD):
        group, at = divmod(head, GROUP)
        lanes = slice(group * 128, group * 128 + 128)
        mine = slice(head * HEAD, head * HEAD + HEAD)
        slot = slice(at * count, at * count + count)

        def padded(block):
            parts = [block]
            if at > 0:
                parts.insert(0, jnp.zeros((at * HEAD, count), BF))
            if at < GROUP - 1:
                parts.append(jnp.zeros(((GROUP - 1 - at) * HEAD, count), BF))
            return jnp.concatenate(parts, axis=0)

        scores = dot(
            jnp.concatenate([key_part[:, lanes], key_mark], axis=1),
            jnp.concatenate([padded(query_t[mine]), query_mark], axis=0),
        )
        dprob = dot(value[:, lanes], padded(dout_t[mine]))
        top = jnp.max(scores, axis=0, keepdims=True)
        expo = jnp.exp(scores - top)
        over = 1.0 / jnp.sum(expo, axis=0, keepdims=True)
        inner = jnp.sum(expo * dprob, axis=0, keepdims=True) * over
        probs = expo * over
        dscore_ref[:, slot] = (probs * (dprob - inner)).astype(BF)
        weights_ref[:, slot] = probs.astype(BF)
        only = (head_of == at).astype(F32).astype(BF)
        query_ref[slot] = query[:, lanes] * only
        dout_ref[slot] = dout[:, lanes] * only
        if at == GROUP - 1:
            dothers_ref[:, lanes] = dot(dscore_ref[...], query_ref[...]).astype(BF)
            dothers_ref[:, slice(width + lanes.start, width + lanes.stop)] = dot(
                weights_ref[...], dout_ref[...]
            ).astype(BF)
            for other in range(GROUP):
                rows = slice(lanes.start + other * HEAD, lanes.start + other * HEAD + HEAD)
                dquery_ref[rows] = dot(
                    key_t[rows], dscore_ref[:, other * count : other * count + count]
                ).astype(BF)

    dnormed = dot(dquery_ref[...], projection[:, :width], ROWS_BY_LAST) + dot(
        dothers_ref[...], projection[:, width:], LAST_BY_LAST
    )
    incoming = dnormed * gain
    mean = jnp.mean(incoming, axis=-1, keepdims=True)
    cross = jnp.mean(incoming * standardized, axis=-1, keepdims=True)
    branch = (inverse * (incoming - mean - standardized * cross)).astype(BF)
    sent_ref[...] = dot(place, branch).astype(BF).reshape(sent_ref.shape)


def post_kernel(got_ref, upper_ref, pick_ref, total_ref):
    branch = dot(pick_ref[...], got_ref[...].reshape(total_ref.shape))
    total_ref[...] = (upper_ref[...].astype(F32) + branch).astype(BF)


def regroup(array):
    return lax.all_to_all(array, "seq", split_axis=0, concat_axis=0, tiled=True)


def per_device(
    block_input,
    upstream,
    w_qkv,
    w_out,
    layer_norm_gain,
    layer_norm_bias,
    send_order,
    recv_order,
    patch_lengths,
):
    _, count, model = block_input.shape
    width = w_out.shape[1]
    peers = lax.axis_size("seq")
    each = count // peers
    sending, placing, lengths = send_order[0], recv_order[0], patch_lengths[0]

    vmem = pl.BlockSpec(memory_space=pltpu.VMEM)
    sent = pl.pallas_call(
        pre_kernel,
        out_shape=jax.ShapeDtypeStruct((peers, each, model + width), BF),
        in_specs=[pl.BlockSpec(memory_space=pltpu.HBM)] * 4,
        out_specs=vmem,
        scratch_shapes=[
            pltpu.VMEM((count, model), BF),
            pltpu.VMEM((count, model), BF),
            pltpu.VMEM((width, model), BF),
            pltpu.VMEM(sending.shape, jnp.int32),
            pltpu.SemaphoreType.DMA((4,)),
        ],
        compiler_params=pltpu.CompilerParams(vmem_limit_bytes=60 * 1024 * 1024),
    )(block_input, upstream, w_out, sending)
    got = regroup(sent)
    upper, pick, place, key_mark, query_mark, gain, shift = pl.pallas_call(
        prepare_kernel,
        out_shape=[
            jax.ShapeDtypeStruct((count, model), BF),
            jax.ShapeDtypeStruct((count, count), BF),
            jax.ShapeDtypeStruct((count, count), BF),
            jax.ShapeDtypeStruct((count, 128), BF),
            jax.ShapeDtypeStruct((128, count), BF),
            jax.ShapeDtypeStruct(layer_norm_gain.shape, F32),
            jax.ShapeDtypeStruct(layer_norm_bias.shape, F32),
        ],
        in_specs=[vmem] * 6,
        out_specs=[vmem] * 7,
        compiler_params=pltpu.CompilerParams(vmem_limit_bytes=8 * 1024 * 1024),
    )(upstream, sending, placing, lengths, layer_norm_gain, layer_norm_bias)
    back = pl.pallas_call(
        main_kernel,
        out_shape=jax.ShapeDtypeStruct((peers, each, model), BF),
        in_specs=[vmem] * 7,
        out_specs=vmem,
        scratch_shapes=[
            pltpu.VMEM((count, GROUP * count), BF),
            pltpu.VMEM((count, GROUP * count), BF),
            pltpu.VMEM((GROUP * count, 128), BF),
            pltpu.VMEM((GROUP * count, 128), BF),
            pltpu.VMEM((width, count), BF),
            pltpu.VMEM((count, 2 * width), BF),
        ],
        compiler_params=pltpu.CompilerParams(vmem_limit_bytes=24 * 1024 * 1024),
    )(got, place, key_mark, query_mark, w_qkv, gain, shift)
    back = regroup(back)
    total = pl.pallas_call(
        post_kernel,
        out_shape=jax.ShapeDtypeStruct((count, model), BF),
        in_specs=[vmem] * 3,
        out_specs=vmem,
        compiler_params=pltpu.CompilerParams(vmem_limit_bytes=8 * 1024 * 1024),
    )(back, upper, pick)
    sections = lax.axis_size("section")
    handed = lax.ppermute(total, "section", [(s, s - 1) for s in range(1, sections)])
    return handed[None]


def solution(mesh):
    return jax.shard_map(
        per_device,
        mesh=mesh,
        in_specs=(
            P("section", "seq", None),
            P("section", "seq", None),
            P("section", None, None),
            P("section", None, None),
            P("section", None),
            P("section", None),
            P("section", "seq", None),
            P("section", "seq", None),
            P("section", "seq", None),
        ),
        out_specs=P("section", "seq", None),
        check_vma=False,
    )
```

time: 81.3 us -> 74.4 us (0.915)
  blocking collectives: 57 us -> 20.9 us
  starting transfers between devices: 1.28 us -> 19.9 us
  waiting for transfers between devices: 6.98 us -> 23.3 us
  Pallas kernels: 13.3 us -> 8.14 us
    all_to_all x2 -> x1, blocking collectives: 57 us -> 20.9 us  [regroup(): return lax.all_to_all(array, 'seq', split_axis=0, concat_axis=0, tiled=True)]
    all_to_all x0 -> x1, starting transfers between devices: none -> 18.6 us  [regroup(): return lax.all_to_all(array, 'seq', split_axis=0, concat_axis=0, tiled=True)]
    all_to_all x0 -> x1, waiting for transfers between devices: none -> 16.6 us  [regroup(): return lax.all_to_all(array, 'seq', split_axis=0, concat_axis=0, tiled=True)]
    pallas_call x1, Pallas kernels: 8.87 us -> 5.18 us  [per_device(): pl.pallas_call(main_kernel, out_shape=jax.ShapeDtypeStruct((peers, each,...]
    pallas_call x1, Pallas kernels: 1.97 us -> 0.23 us  [per_device(): pl.pallas_call(post_kernel, out_shape=jax.ShapeDtypeStruct((count, model)...]
  transfers between devices with their start and end apart: 1 -> 2, of which waited for: 1 -> 2; matrix products, arithmetic and copies ran while one was open for 0% -> 0% of each run, Pallas kernels for 0% -> 0%
where the time goes in v2:
time: 74.4 us; the launch traced here: 73 us
  waiting for transfers between devices  23.3 us (31%)
  blocking collectives  20.9 us (28%)
  starting transfers between devices  19.9 us (27%)
  Pallas kernels  8.14 us (11%)
    all_to_all x1, blocking collectives, regroup(): return lax.all_to_all(array, 'seq', split_axis=0, concat_axis=0, tiled=True)  20.9 us
    all_to_all x1, starting transfers between devices, regroup(): return lax.all_to_all(array, 'seq', split_axis=0, concat_axis=0, tiled=True)  18.6 us
    all_to_all x1, waiting for transfers between devices, regroup(): return lax.all_to_all(array, 'seq', split_axis=0, concat_axis=0, tiled=True)  16.6 us
    ppermute x1, waiting for transfers between devices, per_device(): lax.ppermute(total, 'section', [(s, s - 1) for s in range(1, sections)])  6.7 us
    pallas_call x1, Pallas kernels, per_device(): pl.pallas_call(main_kernel, out_shape=jax.ShapeDtypeStruct((peers, each,...  5.18 us
    pallas_call x1, Pallas kernels, per_device(): pl.pallas_call(pre_kernel, out_shape=jax.ShapeDtypeStruct((peers, each, m...  2.57 us
  transfers between devices with their start and end apart: 2, of which 2 were waited for; matrix products, arithmetic and copies ran while one was open for 0% of the time, Pallas kernels for 0%

profile of v2, /device:TPU:1, one launch (start us, length us, event | category | flops | bytes accessed | tf_op | source)
XLA Modules:
  0.0 73.0 jit_solution(5278097549160090936)
XLA Ops:
  0.0 0.0 copy-start.2
  0.0 0.0 copy-start.3
  0.0 0.0 copy-start.4
  0.0 0.0 copy-start.5
  0.0 0.0 copy-start.6
  0.0 2.6 %shard_map.91 = bf16[128,2,768]{2,1,0:T(2,128)(2,1)} custom-call(bf16[1,256,512]{2,1,0:T(8,128)(2,1)} %rows_hbm.1, bf16[1,256,512]{2,1,0:T(8,128)(2,1)} %upper_in.1, bf16[1,256,512]{2,1,0:T(8,128)(2,1)} %w_out_hbm.1, s32[1,256]{1,0:T(1,128)} %bitcast.4), custom_call_target="tpu_custom_call" | custom-call | tf_op jit(solution)/shard_map/pallas_call | solution.py:201
  2.6 0.0 copy-start
  2.6 0.0 copy-start.1
  2.6 18.6 %all-to-all-start = ((bf16[128,2,768]{2,1,0:T(2,128)(2,1)}), bf16[128,2,768]{2,1,0:T(2,128)(2,1)S(1)}, u32[]{:S(2)}, u32[]{:S(2)}) async-start(bf16[128,2,768]{2,1,0:T(2,128)(2,1)} %shard_map.91), calls=%async_computation | async-start | bytes 786432 | tf_op jit(solution)/shard_map/all_to_all | solution.py:180
  21.2 0.0 copy-done.2
  21.2 0.0 copy-done.3
  21.2 0.0 copy-done.4
  21.2 0.0 copy-done.5
  21.2 0.0 copy-done.6
  21.2 0.0 copy-done
  21.3 0.2 shard_map.92
  21.4 16.6 %all-to-all-done.got_ref = bf16[128,2,768]{2,1,0:T(2,128)(2,1)S(1)} async-done(((bf16[128,2,768]{2,1,0:T(2,128)(2,1)}), bf16[128,2,768]{2,1,0:T(2,128)(2,1)S(1)}, u32[]{:S(2)}, u32[]{:S(2)}) %all-to-all-start) | async-done | bytes 393248 | tf_op jit(solution)/shard_map/all_to_all | solution.py:180
  38.0 0.0 copy-done.1
  38.0 5.2 %shard_map.93 = bf16[128,2,512]{2,1,0:T(2,128)(2,1)S(1)} custom-call(bf16[128,2,768]{2,1,0:T(2,128)(2,1)S(1)} %all-to-all-done.got_ref, bf16[256,256]{1,0:T(8,128)(2,1)S(1)} %get-tuple-element.12.place_ref, bf16[256,128]{1,0:T(8,128)(2,1)S(1)} %get-tuple-element.13.key_mark_ref, bf16[128,256]{1,0:T(8,128)(2,1)S(1)} %get-tuple-element.14.query_mark_ref, ...), custom_call_target="tpu_custom_call" | custom-call | tf_op jit(solution)/shard_map/pallas_call | solution.py:231
  43.2 20.9 %all_to_all.10.got_ref = bf16[128,2,512]{2,1,0:T(2,128)(2,1)S(1)} all-to-all(bf16[128,2,512]{2,1,0:T(2,128)(2,1)S(1)} %shard_map.93), channel_id=1, replica_groups=mesh['seq'=128,'section'=4] {'seq'}, dimensions={0} | all-to-all | bytes 524288 | tf_op jit(solution)/shard_map/all_to_all | solution.py:180
  64.1 0.2 shard_map.94
  64.3 1.3 %collective-permute-start = (bf16[256,512]{1,0:T(8,128)(2,1)S(1)}, bf16[256,512]{1,0:T(8,128)(2,1)S(1)}, u32[]{:S(2)}, u32[]{:S(2)}) collective-permute-start(bf16[256,512]{1,0:T(8,128)(2,1)S(1)} %shard_map.94), channel_id=1, source_target_pairs={{1,0},{2,1},{3,2},{5,4},{6,5},{7,6},{9,8},{10,9},{11,10},{13,12},{... | collective-permute-start | bytes 786440 | tf_op jit(solution)/shard_map/ppermute | solution.py:255
  65.6 6.7 %collective-permute-done = bf16[256,512]{1,0:T(8,128)(2,1)S(1)} collective-permute-done((bf16[256,512]{1,0:T(8,128)(2,1)S(1)}, bf16[256,512]{1,0:T(8,128)(2,1)S(1)}, u32[]{:S(2)}, u32[]{:S(2)}) %collective-permute-start) | collective-permute-done | bytes 262176 | tf_op jit(solution)/shard_map/ppermute | solution.py:255
  72.3 0.7 copy.11
Async XLA Ops:
  0.0 21.2 %copy-start.2 = (s32[1,1,256]{2,1,0:T(1,128)S(1)}, s32[1,1,256]{2,1,0:T(1,128)}, u32[]{:S(2)}) copy-start(s32[1,1,256]{2,1,0:T(1,128)} %param.15) | copy-start | bytes 3076
  0.0 21.2 %copy-start.3 = (f32[1,512]{1,0:T(1,128)S(1)}, f32[1,512]{1,0:T(1,128)}, u32[]{:S(2)}) copy-start(f32[1,512]{1,0:T(1,128)} %gain_in.1) | copy-start | bytes 6148
  0.0 21.2 %copy-start.4 = (f32[1,512]{1,0:T(1,128)S(1)}, f32[1,512]{1,0:T(1,128)}, u32[]{:S(2)}) copy-start(f32[1,512]{1,0:T(1,128)} %shift_in.1) | copy-start | bytes 6148
  0.0 21.2 %copy-start.5 = (s32[1,1,256]{2,1,0:T(1,128)S(1)}, s32[1,1,256]{2,1,0:T(1,128)}, u32[]{:S(2)}) copy-start(s32[1,1,256]{2,1,0:T(1,128)} %param.16) | copy-start | bytes 3076
  0.0 21.2 %copy-start.6 = (s32[1,1,2]{2,1,0:T(1,128)S(1)}, s32[1,1,2]{2,1,0:T(1,128)}, u32[]{:S(2)}) copy-start(s32[1,1,2]{2,1,0:T(1,128)} %param.17) | copy-start | bytes 28
  2.6 18.6 %copy-start = (bf16[1,256,512]{2,1,0:T(8,128)(2,1)S(1)}, bf16[1,256,512]{2,1,0:T(8,128)(2,1)}, u32[]{:S(2)}) copy-start(bf16[1,256,512]{2,1,0:T(8,128)(2,1)} %upper_in.1) | copy-start | bytes 786436
  2.6 35.4 %copy-start.1 = (bf16[1,512,768]{2,1,0:T(8,128)(2,1)S(1)}, bf16[1,512,768]{2,1,0:T(8,128)(2,1)}, u32[]{:S(2)}) copy-start(bf16[1,512,768]{2,1,0:T(8,128)(2,1)} %w_ref.1) | copy-start | bytes 2359300
  2.6 35.4 %all-to-all-start = ((bf16[128,2,768]{2,1,0:T(2,128)(2,1)}), bf16[128,2,768]{2,1,0:T(2,128)(2,1)S(1)}, u32[]{:S(2)}, u32[]{:S(2)}) async-start(bf16[128,2,768]{2,1,0:T(2,128)(2,1)} %shard_map.91), calls=%async_computation | async-start | bytes 786432 | tf_op jit(solution)/shard_map/all_to_all | solution.py:180
  64.3 8.0 %collective-permute-start = (bf16[256,512]{1,0:T(8,128)(2,1)S(1)}, bf16[256,512]{1,0:T(8,128)(2,1)S(1)}, u32[]{:S(2)}, u32[]{:S(2)}) collective-permute-start(bf16[256,512]{1,0:T(8,128)(2,1)S(1)} %shard_map.94), channel_id=1, source_target_pairs={{1,0},{2,1},{3,2},{5,4},{6,5},{7,6},{9,8},{10,9},{11,10},{13,12},{... | collective-permute-start | bytes 786440 | tf_op jit(solution)/shard_map/ppermute | solution.py:255

commit v3 on v2

--- a/solution.py
+++ b/solution.py
@@ -25,36 +25,23 @@
     return jnp.where(wanted == order, 1.0, 0.0).astype(BF)
 
 
+def head_kernel(lanes_ref):
+    owner = lax.broadcasted_iota(jnp.int32, lanes_ref.shape, 1) // HEAD
+    mine = lax.broadcasted_iota(jnp.int32, lanes_ref.shape, 0)
+    lanes_ref[...] = jnp.where(owner == mine, 1.0, 0.0)
+
+
 def pre_kernel(
-    rows_hbm, upper_hbm, w_out_hbm, order_hbm, sent_ref, rows_ref, upper_ref, w_out_ref, order_ref, arrived
-):
-    pairs = [
-        (order_hbm, order_ref),
-        (upper_hbm.at[0], upper_ref),
-        (w_out_hbm.at[0], w_out_ref),
-        (rows_hbm.at[0], rows_ref),
-    ]
-    copies = [pltpu.make_async_copy(a, b, arrived.at[i]) for i, (a, b) in enumerate(pairs)]
-    for copy in copies:
-        copy.start()
-    copies[0].wait()
-    pick = selection(order_ref[...])
-    copies[1].wait()
-    copies[2].wait()
-    out_common = dot(upper_ref[...], w_out_ref[...], LAST_BY_LAST).astype(BF)
-    copies[3].wait()
-    both = jnp.concatenate([rows_ref[...], out_common], axis=1)
-    sent_ref[...] = dot(pick, both, ROWS_BY_ROWS).astype(BF).reshape(sent_ref.shape)
-
-
-def prepare_kernel(
-    upper_in,
-    sending_in,
-    placing_in,
-    lengths_in,
+    rows_ref,
+    upper_ref,
+    w_out_ref,
+    sending_ref,
+    placing_ref,
+    lengths_ref,
     gain_in,
     shift_in,
-    upper_ref,
+    _,
+    sent_ref,
     pick_ref,
     place_ref,
     key_mark_ref,
@@ -62,13 +49,17 @@
     gain_ref,
     shift_ref,
 ):
-    upper_ref[...] = upper_in[0]
-    pick_ref[...] = selection(sending_in[...])
-    place_ref[...] = selection(placing_in[...])
+    pick = selection(sending_ref[...])
+    pick_ref[...] = pick
+    out_common = dot(upper_ref[0], w_out_ref[0], LAST_BY_LAST).astype(BF)
+    both = jnp.concatenate([rows_ref[0], out_common], axis=1)
+    sent_ref[...] = dot(pick, both, ROWS_BY_ROWS).astype(BF).reshape(sent_ref.shape)
+
+    place_ref[...] = selection(placing_ref[...])
     gain_ref[...] = gain_in[...]
     shift_ref[...] = shift_in[...]
-    first = lengths_in[:, :1]
-    count = placing_in.shape[1]
+    first = lengths_ref[:, :1]
+    count = placing_ref.shape[1]
     key_at = (lax.broadcasted_iota(jnp.int32, (count, 128), 0) < first).astype(jnp.int32)
     lane = lax.broadcasted_iota(jnp.int32, (count, 128), 1)
     key_mark_ref[...] = jnp.where(lane == key_at, 1.0, 0.0).astype(BF)
@@ -85,6 +76,7 @@
     w_ref,
     gain_ref,
     shift_ref,
+    head_lanes_ref,
     sent_ref,
     dscore_ref,
     weights_ref,
@@ -119,7 +111,6 @@
 
     key_mark = key_mark_ref[...]
     query_mark = query_mark_ref[...]
-    head_of = lax.broadcasted_iota(jnp.int32, (count, 128), 1) // HEAD
 
     for head in range(width // HEAD):
         group, at = divmod(head, GROUP)
@@ -147,7 +138,7 @@
         probs = expo * over
         dscore_ref[:, slot] = (probs * (dprob - inner)).astype(BF)
         weights_ref[:, slot] = probs.astype(BF)
-        only = (head_of == at).astype(F32).astype(BF)
+        only = head_lanes_ref[at : at + 1].astype(BF)
         query_ref[slot] = query[:, lanes] * only
         dout_ref[slot] = dout[:, lanes] * only
         if at == GROUP - 1:
@@ -173,7 +164,7 @@
 
 def post_kernel(got_ref, upper_ref, pick_ref, total_ref):
     branch = dot(pick_ref[...], got_ref[...].reshape(total_ref.shape))
-    total_ref[...] = (upper_ref[...].astype(F32) + branch).astype(BF)
+    total_ref[...] = (upper_ref[0].astype(F32) + branch).astype(BF)
 
 
 def regroup(array):
@@ -198,25 +189,18 @@
     sending, placing, lengths = send_order[0], recv_order[0], patch_lengths[0]
 
     vmem = pl.BlockSpec(memory_space=pltpu.VMEM)
-    sent = pl.pallas_call(
+    small = pltpu.CompilerParams(vmem_limit_bytes=8 * 1024 * 1024)
+    head_lanes = pl.pallas_call(
+        head_kernel,
+        out_shape=jax.ShapeDtypeStruct((GROUP, 128), F32),
+        out_specs=vmem,
+        compiler_params=small,
+        cost_estimate=pl.CostEstimate(flops=10**10, transcendentals=0, bytes_accessed=10**7),
+    )()
+    sent, pick, place, key_mark, query_mark, gain, shift = pl.pallas_call(
         pre_kernel,
-        out_shape=jax.ShapeDtypeStruct((peers, each, model + width), BF),
-        in_specs=[pl.BlockSpec(memory_space=pltpu.HBM)] * 4,
-        out_specs=vmem,
-        scratch_shapes=[
-            pltpu.VMEM((count, model), BF),
-            pltpu.VMEM((count, model), BF),
-            pltpu.VMEM((width, model), BF),
-            pltpu.VMEM(sending.shape, jnp.int32),
-            pltpu.SemaphoreType.DMA((4,)),
-        ],
-        compiler_params=pltpu.CompilerParams(vmem_limit_bytes=60 * 1024 * 1024),
-    )(block_input, upstream, w_out, sending)
-    got = regroup(sent)
-    upper, pick, place, key_mark, query_mark, gain, shift = pl.pallas_call(
-        prepare_kernel,
         out_shape=[
-            jax.ShapeDtypeStruct((count, model), BF),
+            jax.ShapeDtypeStruct((peers, each, model + width), BF),
             jax.ShapeDtypeStruct((count, count), BF),
             jax.ShapeDtypeStruct((count, count), BF),
             jax.ShapeDtypeStruct((count, 128), BF),
@@ -224,14 +208,25 @@
             jax.ShapeDtypeStruct(layer_norm_gain.shape, F32),
             jax.ShapeDtypeStruct(layer_norm_bias.shape, F32),
         ],
-        in_specs=[vmem] * 6,
+        in_specs=[vmem] * 9,
         out_specs=[vmem] * 7,
-        compiler_params=pltpu.CompilerParams(vmem_limit_bytes=8 * 1024 * 1024),
-    )(upstream, sending, placing, lengths, layer_norm_gain, layer_norm_bias)
+        compiler_params=small,
+    )(
+        block_input,
+        upstream,
+        w_out,
+        sending,
+        placing,
+        lengths,
+        layer_norm_gain,
+        layer_norm_bias,
+        head_lanes,
+    )
+    got = regroup(sent)
     back = pl.pallas_call(
         main_kernel,
         out_shape=jax.ShapeDtypeStruct((peers, each, model), BF),
-        in_specs=[vmem] * 7,
+        in_specs=[vmem] * 8,
         out_specs=vmem,
         scratch_shapes=[
             pltpu.VMEM((count, GROUP * count), BF),
@@ -242,7 +237,7 @@
             pltpu.VMEM((count, 2 * width), BF),
         ],
         compiler_params=pltpu.CompilerParams(vmem_limit_bytes=24 * 1024 * 1024),
-    )(got, place, key_mark, query_mark, w_qkv, gain, shift)
+    )(got, place, key_mark, query_mark, w_qkv, gain, shift, head_lanes)
     back = regroup(back)
     total = pl.pallas_call(
         post_kernel,
@@ -250,7 +245,7 @@
         in_specs=[vmem] * 3,
         out_specs=vmem,
         compiler_params=pltpu.CompilerParams(vmem_limit_bytes=8 * 1024 * 1024),
-    )(back, upper, pick)
+    )(back, upstream, pick)
     sections = lax.axis_size("section")
     handed = lax.ppermute(total, "section", [(s, s - 1) for s in range(1, sections)])
     return handed[None]

time: 74.4 us -> 73.1 us (0.983)
  blocking collectives: 20.9 us -> 55.9 us
  starting transfers between devices: 19.9 us -> 1.29 us
  waiting for transfers between devices: 23.3 us -> 6.7 us
  Pallas kernels: 8.14 us -> 6.03 us
  local copies, waits for them, and re-layouts: 0.73 us -> 1.77 us
    all_to_all x1 -> x2, blocking collectives: 20.9 us -> 55.9 us  [regroup(): return lax.all_to_all(array, 'seq', split_axis=0, concat_axis=0, tiled=True)]
    all_to_all x1 -> x0, starting transfers between devices: 18.6 us -> none  [regroup(): return lax.all_to_all(array, 'seq', split_axis=0, concat_axis=0, tiled=True)]
    all_to_all x1 -> x0, waiting for transfers between devices: 16.6 us -> none  [regroup(): return lax.all_to_all(array, 'seq', split_axis=0, concat_axis=0, tiled=True)]
    pallas_call x2, Pallas kernels: 2.73 us -> 0.56 us  [the longest x1 0.55 us: per_device(): pl.pallas_call(pre_kernel, out_shape=[jax.ShapeDtypeStruct((peers, each,...]
    unnamed x15 -> x19, local copies, waits for them, and re-layouts: 0.73 us -> 1.77 us
  transfers between devices with their start and end apart: 2 -> 1, of which waited for: 2 -> 1; matrix products, arithmetic and copies ran while one was open for 0% -> 0% of each run, Pallas kernels for 0% -> 0%
where the time goes in v3:
time: 73.1 us; the launch traced here: 71.8 us
  blocking collectives  55.9 us (76%)
  waiting for transfers between devices  6.7 us (9%)
  Pallas kernels  6.03 us (8%)
  local copies, waits for them, and re-layouts  1.77 us (2%)
  starting transfers between devices  1.29 us (2%)
    all_to_all x2, blocking collectives, regroup(): return lax.all_to_all(array, 'seq', split_axis=0, concat_axis=0, tiled=True)  55.9 us
    ppermute x1, waiting for transfers between devices, per_device(): lax.ppermute(total, 'section', [(s, s - 1) for s in range(1, sections)])  6.7 us
    pallas_call x1, Pallas kernels, per_device(): pl.pallas_call(main_kernel, out_shape=jax.ShapeDtypeStruct((peers, each,...  5.23 us
    unnamed x19, local copies, waits for them, and re-layouts  1.77 us
  transfers between devices with their start and end apart: 1, of which 1 were waited for; matrix products, arithmetic and copies ran while one was open for 0% of the time, Pallas kernels for 0%

profile of v3, /device:TPU:1, one launch (start us, length us, event | category | flops | bytes accessed | tf_op | source)
XLA Modules:
  0.0 71.8 jit_solution(6441112433184526575)
XLA Ops:
  0.0 0.0 copy-start
  0.0 0.0 copy-start.3
  0.0 0.0 copy-start.2
  0.0 0.0 copy-start.7
  0.0 0.0 copy-start.5
  0.0 0.0 copy-start.4
  0.1 0.0 copy-start.6
  0.1 0.0 copy-start.8
  0.1 0.9 %copy-done = bf16[1,256,512]{2,1,0:T(8,128)(2,1)S(1)} copy-done((bf16[1,256,512]{2,1,0:T(8,128)(2,1)S(1)}, bf16[1,256,512]{2,1,0:T(8,128)(2,1)}, u32[]{:S(2)}) %copy-start) | copy-done | bytes 262168
  1.0 0.1 copy-done.3
  1.0 0.1 copy-done.2
  1.1 0.0 copy-done.7
  1.1 0.0 copy-done.5
  1.1 0.0 copy-done.4
  1.1 0.0 copy-done.6
  1.1 0.0 copy-done.8
  1.1 0.0 copy-start.1
  1.1 0.6 shard_map.92
  1.7 35.0 %all_to_all.10.got_ref = bf16[128,2,768]{2,1,0:T(2,128)(2,1)S(1)} all-to-all(bf16[128,2,768]{2,1,0:T(2,128)(2,1)S(1)} %get-tuple-element.12), channel_id=1, replica_groups=mesh['seq'=128,'section'=4] {'seq'}, dimensions={0} | all-to-all | bytes 786432 | tf_op jit(solution)/shard_map/all_to_all | solution.py:171
  36.7 0.0 copy-done.1
  36.7 5.2 %shard_map.93 = bf16[128,2,512]{2,1,0:T(2,128)(2,1)S(1)} custom-call(bf16[128,2,768]{2,1,0:T(2,128)(2,1)S(1)} %all_to_all.10.got_ref, bf16[256,256]{1,0:T(8,128)(2,1)S(1)} %get-tuple-element.13.place_ref, bf16[256,128]{1,0:T(8,128)(2,1)S(1)} %get-tuple-element.14.key_mark_ref, bf16[128,256]{1,0:T(8,128)(2,1)S(1)} %get-tuple-element.15.query_mark_ref, ...), custom_call_target="tpu_custom_call" | custom-call | tf_op jit(solution)/shard_map/pallas_call | solution.py:226
  42.0 20.9 %all_to_all.11.got_ref = bf16[128,2,512]{2,1,0:T(2,128)(2,1)S(1)} all-to-all(bf16[128,2,512]{2,1,0:T(2,128)(2,1)S(1)} %shard_map.93), channel_id=1, replica_groups=mesh['seq'=128,'section'=4] {'seq'}, dimensions={0} | all-to-all | bytes 524288 | tf_op jit(solution)/shard_map/all_to_all | solution.py:171
  62.9 0.2 shard_map.94
  63.1 1.3 %collective-permute-start = (bf16[256,512]{1,0:T(8,128)(2,1)S(1)}, bf16[256,512]{1,0:T(8,128)(2,1)S(1)}, u32[]{:S(2)}, u32[]{:S(2)}) collective-permute-start(bf16[256,512]{1,0:T(8,128)(2,1)S(1)} %shard_map.94), channel_id=1, source_target_pairs={{1,0},{2,1},{3,2},{5,4},{6,5},{7,6},{9,8},{10,9},{11,10},{13,12},{... | collective-permute-start | bytes 786440 | tf_op jit(solution)/shard_map/ppermute | solution.py:250
  64.4 6.7 %collective-permute-done = bf16[256,512]{1,0:T(8,128)(2,1)S(1)} collective-permute-done((bf16[256,512]{1,0:T(8,128)(2,1)S(1)}, bf16[256,512]{1,0:T(8,128)(2,1)S(1)}, u32[]{:S(2)}, u32[]{:S(2)}) %collective-permute-start) | collective-permute-done | bytes 262176 | tf_op jit(solution)/shard_map/ppermute | solution.py:250
  71.1 0.7 copy.11
  (1 shorter events, 0.0 us)
Async XLA Ops:
  0.0 0.9 %copy-start = (bf16[1,256,512]{2,1,0:T(8,128)(2,1)S(1)}, bf16[1,256,512]{2,1,0:T(8,128)(2,1)}, u32[]{:S(2)}) copy-start(bf16[1,256,512]{2,1,0:T(8,128)(2,1)} %upper_ref.3) | copy-start | bytes 786436
  0.0 1.0 %copy-start.3 = (bf16[1,256,512]{2,1,0:T(8,128)(2,1)S(1)}, bf16[1,256,512]{2,1,0:T(8,128)(2,1)}, u32[]{:S(2)}) copy-start(bf16[1,256,512]{2,1,0:T(8,128)(2,1)} %w_out_ref.1) | copy-start | bytes 786436
  0.0 1.1 %copy-start.2 = (bf16[1,256,512]{2,1,0:T(8,128)(2,1)S(1)}, bf16[1,256,512]{2,1,0:T(8,128)(2,1)}, u32[]{:S(2)}) copy-start(bf16[1,256,512]{2,1,0:T(8,128)(2,1)} %rows_ref.1) | copy-start | bytes 786436
  0.0 1.1 %copy-start.7 = (s32[1,1,256]{2,1,0:T(1,128)S(1)}, s32[1,1,256]{2,1,0:T(1,128)}, u32[]{:S(2)}) copy-start(s32[1,1,256]{2,1,0:T(1,128)} %param.16) | copy-start | bytes 3076
  0.0 1.1 %copy-start.5 = (f32[1,512]{1,0:T(1,128)S(1)}, f32[1,512]{1,0:T(1,128)}, u32[]{:S(2)}) copy-start(f32[1,512]{1,0:T(1,128)} %shift_in.1) | copy-start | bytes 6148
  0.0 1.1 %copy-start.4 = (f32[1,512]{1,0:T(1,128)S(1)}, f32[1,512]{1,0:T(1,128)}, u32[]{:S(2)}) copy-start(f32[1,512]{1,0:T(1,128)} %gain_in.1) | copy-start | bytes 6148
  0.1 1.1 %copy-start.6 = (s32[1,1,256]{2,1,0:T(1,128)S(1)}, s32[1,1,256]{2,1,0:T(1,128)}, u32[]{:S(2)}) copy-start(s32[1,1,256]{2,1,0:T(1,128)} %param.15) | copy-start | bytes 3076
  0.1 1.1 %copy-start.8 = (s32[1,1,2]{2,1,0:T(1,128)S(1)}, s32[1,1,2]{2,1,0:T(1,128)}, u32[]{:S(2)}) copy-start(s32[1,1,2]{2,1,0:T(1,128)} %param.17) | copy-start | bytes 28
  1.1 35.6 %copy-start.1 = (bf16[1,512,768]{2,1,0:T(8,128)(2,1)S(1)}, bf16[1,512,768]{2,1,0:T(8,128)(2,1)}, u32[]{:S(2)}) copy-start(bf16[1,512,768]{2,1,0:T(8,128)(2,1)} %w_ref.1) | copy-start | bytes 2359300
  63.1 8.0 %collective-permute-start = (bf16[256,512]{1,0:T(8,128)(2,1)S(1)}, bf16[256,512]{1,0:T(8,128)(2,1)S(1)}, u32[]{:S(2)}, u32[]{:S(2)}) collective-permute-start(bf16[256,512]{1,0:T(8,128)(2,1)S(1)} %shard_map.94), channel_id=1, source_target_pairs={{1,0},{2,1},{3,2},{5,4},{6,5},{7,6},{9,8},{10,9},{11,10},{13,12},{... | collective-permute-start | bytes 786440 | tf_op jit(solution)/shard_map/ppermute | solution.py:250

commit v4 on v3

v4 whole, which is shorter than its diff:
```python
import jax
import jax.numpy as jnp
from jax import lax
from jax.experimental import pallas as pl
from jax.experimental.pallas import tpu as pltpu
from jax.sharding import PartitionSpec as P

HEAD = 16
MASKED = -(2.0**99)
BF = jnp.bfloat16
F32 = jnp.float32
ROWS_BY_ROWS = (((0,), (0,)), ((), ()))
LAST_BY_LAST = (((1,), (1,)), ((), ()))
ROWS_BY_LAST = (((0,), (1,)), ((), ()))


def dot(a, b, dims=(((1,), (0,)), ((), ()))):
    return lax.dot_general(a, b, dims, preferred_element_type=F32)


def selection(numbers, order):
    return jnp.where(numbers == order, 1.0, 0.0).astype(BF)


def number_kernel(numbers_ref):
    numbers_ref[...] = lax.broadcasted_iota(jnp.int32, numbers_ref.shape, 0)


def pre_kernel(
    rows_ref,
    upper_ref,
    w_out_ref,
    sending_ref,
    placing_ref,
    lengths_ref,
    gain_in,
    shift_in,
    numbers_ref,
    sent_ref,
    pick_ref,
    place_ref,
    key_mark_ref,
    query_mark_ref,
    gain_ref,
    shift_ref,
):
    pick = selection(numbers_ref[...], sending_ref[...])
    pick_ref[...] = pick
    out_common = dot(upper_ref[0], w_out_ref[0], LAST_BY_LAST).astype(BF)
    both = jnp.concatenate([rows_ref[0], out_common], axis=1)
    sent_ref[...] = dot(pick, both, ROWS_BY_ROWS).astype(BF).reshape(sent_ref.shape)

    place_ref[...] = selection(numbers_ref[...], placing_ref[...])
    gain_ref[...] = gain_in[...]
    shift_ref[...] = shift_in[...]
    first = lengths_ref[:, :1]
    count = placing_ref.shape[1]
    key_at = (lax.broadcasted_iota(jnp.int32, (count, HEAD), 0) < first).astype(jnp.int32)
    lane = lax.broadcasted_iota(jnp.int32, (count, HEAD), 1)
    key_mark_ref[...] = jnp.where(lane == key_at, 1.0, 0.0).astype(BF)
    query_at = (lax.broadcasted_iota(jnp.int32, (HEAD, count), 1) >= first).astype(jnp.int32)
    sub = lax.broadcasted_iota(jnp.int32, (HEAD, count), 0)
    query_mark_ref[...] = jnp.where(sub == query_at, MASKED, 0.0).astype(BF)


def main_kernel(
    got_ref,
    place_ref,
    key_mark_ref,
    query_mark_ref,
    w_ref,
    gain_ref,
    shift_ref,
    sent_ref,
    dscore_ref,
    weights_ref,
    grads_ref,
):
    count = place_ref.shape[0]
    projection = w_ref[0]
    model = projection.shape[0]
    width = projection.shape[1] // 3
    gain = gain_ref[...]
    place = place_ref[...]
    got = dot(place, got_ref[...].reshape(count, model + width), ROWS_BY_ROWS)

    values = got[:, :model]
    centered = values - jnp.mean(values, axis=-1, keepdims=True)
    inverse = lax.rsqrt(jnp.mean(centered * centered, axis=-1, keepdims=True) + 1e-05)
    standardized = centered * inverse
    normed = (standardized * gain + shift_ref[...]).astype(BF)
    qkv = dot(normed, projection).astype(BF)
    dout = got[:, model:].astype(BF)

    scale = float(HEAD) ** (-0.5)
    query = qkv[:, :width] * scale
    key_part = qkv[:, width : 2 * width]
    value = qkv[:, 2 * width :]
    query_t = query.T
    key_t = (key_part * scale).T
    dout_t = dout.T

    key_mark = key_mark_ref[...]
    query_mark = query_mark_ref[...]

    for head in range(width // HEAD):
        mine = slice(head * HEAD, head * HEAD + HEAD)
        slot = slice(head * count, head * count + count)
        scores = dot(
            jnp.concatenate([key_part[:, mine], key_mark], axis=1),
            jnp.concatenate([query_t[mine], query_mark], axis=0),
        )
        dprob = dot(value[:, mine], dout_t[mine])
        top = jnp.max(scores, axis=0, keepdims=True)
        expo = jnp.exp(scores - top)
        over = 1.0 / jnp.sum(expo, axis=0, keepdims=True)
        inner = jnp.sum(expo * dprob, axis=0, keepdims=True) * over
        probs = expo * over
        dscore_ref[:, slot] = (probs * (dprob - inner)).astype(BF)
        weights_ref[:, slot] = probs.astype(BF)

    for head in range(width // HEAD):
        query_rows = slice(head * HEAD, head * HEAD + HEAD)
        key_rows = slice(width + query_rows.start, width + query_rows.stop)
        value_rows = slice(width + key_rows.start, width + key_rows.stop)
        slot = slice(head * count, head * count + count)
        dscore = dscore_ref[:, slot]
        grads_ref[query_rows] = dot(key_t[query_rows], dscore).astype(BF)
        grads_ref[key_rows] = dot(query_t[query_rows], dscore, LAST_BY_LAST).astype(BF)
        grads_ref[value_rows] = dot(dout_t[query_rows], weights_ref[:, slot], LAST_BY_LAST).astype(BF)

    dnormed = dot(grads_ref[...], projection, ROWS_BY_LAST)
    incoming = dnormed * gain
    mean = jnp.mean(incoming, axis=-1, keepdims=True)
    cross = jnp.mean(incoming * standardized, axis=-1, keepdims=True)
    branch = (inverse * (incoming - mean - standardized * cross)).astype(BF)
    sent_ref[...] = dot(place, branch).astype(BF).reshape(sent_ref.shape)


def post_kernel(got_ref, upper_ref, pick_ref, total_ref):
    branch = dot(pick_ref[...], got_ref[...].reshape(total_ref.shape))
    total_ref[...] = (upper_ref[0].astype(F32) + branch).astype(BF)


def regroup(array):
    return lax.all_to_all(array, "seq", split_axis=0, concat_axis=0, tiled=True)


def per_device(
    block_input,
    upstream,
    w_qkv,
    w_out,
    layer_norm_gain,
    layer_norm_bias,
    send_order,
    recv_order,
    patch_lengths,
):
    _, count, model = block_input.shape
    width = w_out.shape[1]
    peers = lax.axis_size("seq")
    each = count // peers
    sending, placing, lengths = send_order[0], recv_order[0], patch_lengths[0]

    vmem = pl.BlockSpec(memory_space=pltpu.VMEM)
    small = pltpu.CompilerParams(vmem_limit_bytes=8 * 1024 * 1024)
    numbers = pl.pallas_call(
        number_kernel,
        out_shape=jax.ShapeDtypeStruct((count, count), jnp.int32),
        out_specs=vmem,
        compiler_params=small,
        cost_estimate=pl.CostEstimate(flops=10**10, transcendentals=0, bytes_accessed=10**7),
    )()
    sent, pick, place, key_mark, query_mark, gain, shift = pl.pallas_call(
        pre_kernel,
        out_shape=[
            jax.ShapeDtypeStruct((peers, each, model + width), BF),
            jax.ShapeDtypeStruct((count, count), BF),
            jax.ShapeDtypeStruct((count, count), BF),
            jax.ShapeDtypeStruct((count, HEAD), BF),
            jax.ShapeDtypeStruct((HEAD, count), BF),
            jax.ShapeDtypeStruct(layer_norm_gain.shape, F32),
            jax.ShapeDtypeStruct(layer_norm_bias.shape, F32),
        ],
        in_specs=[vmem] * 9,
        out_specs=[vmem] * 7,
        compiler_params=small,
    )(
        block_input,
        upstream,
        w_out,
        sending,
        placing,
        lengths,
        layer_norm_gain,
        layer_norm_bias,
        numbers,
    )
    got = regroup(sent)
    back = pl.pallas_call(
        main_kernel,
        out_shape=jax.ShapeDtypeStruct((peers, each, model), BF),
        in_specs=[vmem] * 7,
        out_specs=vmem,
        scratch_shapes=[
            pltpu.VMEM((count, width // HEAD * count), BF),
            pltpu.VMEM((count, width // HEAD * count), BF),
            pltpu.VMEM((3 * width, count), BF),
        ],
        compiler_params=pltpu.CompilerParams(vmem_limit_bytes=24 * 1024 * 1024),
    )(got, place, key_mark, query_mark, w_qkv, gain, shift)
    back = regroup(back)
    total = pl.pallas_call(
        post_kernel,
        out_shape=jax.ShapeDtypeStruct((count, model), BF),
        in_specs=[vmem] * 3,
        out_specs=vmem,
        compiler_params=pltpu.CompilerParams(vmem_limit_bytes=8 * 1024 * 1024),
    )(back, upstream, pick)
    sections = lax.axis_size("section")
    handed = lax.ppermute(total, "section", [(s, s - 1) for s in range(1, sections)])
    return handed[None]


def solution(mesh):
    return jax.shard_map(
        per_device,
        mesh=mesh,
        in_specs=(
            P("section", "seq", None),
            P("section", "seq", None),
            P("section", None, None),
            P("section", None, None),
            P("section", None),
            P("section", None),
            P("section", "seq", None),
            P("section", "seq", None),
            P("section", "seq", None),
        ),
        out_specs=P("section", "seq", None),
        check_vma=False,
    )
```

time: 73.1 us -> 72.4 us (level)
    pallas_call x1, Pallas kernels: 5.23 us -> 4.5 us  [per_device(): pl.pallas_call(main_kernel, out_shape=jax.ShapeDtypeStruct((peers, each,...]
where the time goes in v4:
time: 72.4 us; the launch traced here: 71.1 us
  blocking collectives  55.9 us (77%)
  waiting for transfers between devices  6.71 us (9%)
  Pallas kernels  5.32 us (7%)
  local copies, waits for them, and re-layouts  1.76 us (2%)
  starting transfers between devices  1.29 us (2%)
    all_to_all x2, blocking collectives, regroup(): return lax.all_to_all(array, 'seq', split_axis=0, concat_axis=0, tiled=True)  55.9 us
    ppermute x1, waiting for transfers between devices, per_device(): lax.ppermute(total, 'section', [(s, s - 1) for s in range(1, sections)])  6.71 us
    pallas_call x1, Pallas kernels, per_device(): pl.pallas_call(main_kernel, out_shape=jax.ShapeDtypeStruct((peers, each,...  4.5 us
    unnamed x19, local copies, waits for them, and re-layouts  1.76 us
  transfers between devices with their start and end apart: 1, of which 1 were waited for; matrix products, arithmetic and copies ran while one was open for 0% of the time, Pallas kernels for 0%

profile of v4, /device:TPU:1, one launch (start us, length us, event | category | flops | bytes accessed | tf_op | source)
XLA Modules:
  0.0 71.1 jit_solution(10444210276174724653)
XLA Ops:
  0.0 0.0 copy-start
  0.0 0.0 copy-start.3
  0.0 0.0 copy-start.2
  0.0 0.0 copy-start.7
  0.0 0.0 copy-start.5
  0.1 0.0 copy-start.4
  0.1 0.0 copy-start.6
  0.1 0.0 copy-start.8
  0.1 0.9 %copy-done = bf16[1,256,512]{2,1,0:T(8,128)(2,1)S(1)} copy-done((bf16[1,256,512]{2,1,0:T(8,128)(2,1)S(1)}, bf16[1,256,512]{2,1,0:T(8,128)(2,1)}, u32[]{:S(2)}) %copy-start) | copy-done | bytes 262168
  1.0 0.1 copy-done.3
  1.0 0.1 copy-done.2
  1.1 0.0 copy-done.7
  1.1 0.0 copy-done.5
  1.1 0.0 copy-done.4
  1.1 0.0 copy-done.6
  1.1 0.0 copy-done.8
  1.1 0.0 copy-start.1
  1.1 0.6 shard_map.92
  1.7 35.0 %all_to_all.10.got_ref = bf16[128,2,768]{2,1,0:T(2,128)(2,1)S(1)} all-to-all(bf16[128,2,768]{2,1,0:T(2,128)(2,1)S(1)} %get-tuple-element.12), channel_id=1, replica_groups=mesh['seq'=128,'section'=4] {'seq'}, dimensions={0} | all-to-all | bytes 786432 | tf_op jit(solution)/shard_map/all_to_all | solution.py:146
  36.7 0.0 copy-done.1
  36.7 4.5 %shard_map.93 = bf16[128,2,512]{2,1,0:T(2,128)(2,1)S(1)} custom-call(bf16[128,2,768]{2,1,0:T(2,128)(2,1)S(1)} %all_to_all.10.got_ref, bf16[256,256]{1,0:T(8,128)(2,1)S(1)} %get-tuple-element.13.place_ref, bf16[256,16]{1,0:T(8,128)(2,1)S(1)} %get-tuple-element.14.key_mark_ref, bf16[16,256]{1,0:T(8,128)(2,1)S(1)} %get-tuple-element.15.query_mark_ref, ...), custom_call_target="tpu_custom_call" | custom-call | tf_op jit(solution)/shard_map/pallas_call | solution.py:201
  41.3 20.9 %all_to_all.11.got_ref = bf16[128,2,512]{2,1,0:T(2,128)(2,1)S(1)} all-to-all(bf16[128,2,512]{2,1,0:T(2,128)(2,1)S(1)} %shard_map.93), channel_id=1, replica_groups=mesh['seq'=128,'section'=4] {'seq'}, dimensions={0} | all-to-all | bytes 524288 | tf_op jit(solution)/shard_map/all_to_all | solution.py:146
  62.2 0.2 shard_map.94
  62.4 1.3 %collective-permute-start = (bf16[256,512]{1,0:T(8,128)(2,1)S(1)}, bf16[256,512]{1,0:T(8,128)(2,1)S(1)}, u32[]{:S(2)}, u32[]{:S(2)}) collective-permute-start(bf16[256,512]{1,0:T(8,128)(2,1)S(1)} %shard_map.94), channel_id=1, source_target_pairs={{1,0},{2,1},{3,2},{5,4},{6,5},{7,6},{9,8},{10,9},{11,10},{13,12},{... | collective-permute-start | bytes 786440 | tf_op jit(solution)/shard_map/ppermute | solution.py:222
  63.7 6.7 %collective-permute-done = bf16[256,512]{1,0:T(8,128)(2,1)S(1)} collective-permute-done((bf16[256,512]{1,0:T(8,128)(2,1)S(1)}, bf16[256,512]{1,0:T(8,128)(2,1)S(1)}, u32[]{:S(2)}, u32[]{:S(2)}) %collective-permute-start) | collective-permute-done | bytes 262176 | tf_op jit(solution)/shard_map/ppermute | solution.py:222
  70.4 0.7 copy.11
  (1 shorter events, 0.0 us)
Async XLA Ops:
  0.0 0.9 %copy-start = (bf16[1,256,512]{2,1,0:T(8,128)(2,1)S(1)}, bf16[1,256,512]{2,1,0:T(8,128)(2,1)}, u32[]{:S(2)}) copy-start(bf16[1,256,512]{2,1,0:T(8,128)(2,1)} %upper_ref.3) | copy-start | bytes 786436
  0.0 1.0 %copy-start.3 = (bf16[1,256,512]{2,1,0:T(8,128)(2,1)S(1)}, bf16[1,256,512]{2,1,0:T(8,128)(2,1)}, u32[]{:S(2)}) copy-start(bf16[1,256,512]{2,1,0:T(8,128)(2,1)} %w_out_ref.1) | copy-start | bytes 786436
  0.0 1.1 %copy-start.2 = (bf16[1,256,512]{2,1,0:T(8,128)(2,1)S(1)}, bf16[1,256,512]{2,1,0:T(8,128)(2,1)}, u32[]{:S(2)}) copy-start(bf16[1,256,512]{2,1,0:T(8,128)(2,1)} %rows_ref.1) | copy-start | bytes 786436
  0.0 1.1 %copy-start.7 = (s32[1,1,256]{2,1,0:T(1,128)S(1)}, s32[1,1,256]{2,1,0:T(1,128)}, u32[]{:S(2)}) copy-start(s32[1,1,256]{2,1,0:T(1,128)} %param.16) | copy-start | bytes 3076
  0.0 1.1 %copy-start.5 = (f32[1,512]{1,0:T(1,128)S(1)}, f32[1,512]{1,0:T(1,128)}, u32[]{:S(2)}) copy-start(f32[1,512]{1,0:T(1,128)} %shift_in.1) | copy-start | bytes 6148
  0.1 1.1 %copy-start.4 = (f32[1,512]{1,0:T(1,128)S(1)}, f32[1,512]{1,0:T(1,128)}, u32[]{:S(2)}) copy-start(f32[1,512]{1,0:T(1,128)} %gain_in.1) | copy-start | bytes 6148
  0.1 1.0 %copy-start.6 = (s32[1,1,256]{2,1,0:T(1,128)S(1)}, s32[1,1,256]{2,1,0:T(1,128)}, u32[]{:S(2)}) copy-start(s32[1,1,256]{2,1,0:T(1,128)} %param.15) | copy-start | bytes 3076
  0.1 1.0 %copy-start.8 = (s32[1,1,2]{2,1,0:T(1,128)S(1)}, s32[1,1,2]{2,1,0:T(1,128)}, u32[]{:S(2)}) copy-start(s32[1,1,2]{2,1,0:T(1,128)} %param.17) | copy-start | bytes 28
  1.1 35.6 %copy-start.1 = (bf16[1,512,768]{2,1,0:T(8,128)(2,1)S(1)}, bf16[1,512,768]{2,1,0:T(8,128)(2,1)}, u32[]{:S(2)}) copy-start(bf16[1,512,768]{2,1,0:T(8,128)(2,1)} %w_ref.1) | copy-start | bytes 2359300
  62.4 8.0 %collective-permute-start = (bf16[256,512]{1,0:T(8,128)(2,1)S(1)}, bf16[256,512]{1,0:T(8,128)(2,1)S(1)}, u32[]{:S(2)}, u32[]{:S(2)}) collective-permute-start(bf16[256,512]{1,0:T(8,128)(2,1)S(1)} %shard_map.94), channel_id=1, source_target_pairs={{1,0},{2,1},{3,2},{5,4},{6,5},{7,6},{9,8},{10,9},{11,10},{13,12},{... | collective-permute-start | bytes 786440 | tf_op jit(solution)/shard_map/ppermute | solution.py:222

commit v5 on v4

--- a/solution.py
+++ b/solution.py
@@ -1,3 +1,5 @@
+import functools
+
 import jax
 import jax.numpy as jnp
 from jax import lax
@@ -6,6 +8,7 @@
 from jax.sharding import PartitionSpec as P
 
 HEAD = 16
+FIRST = 72
 MASKED = -(2.0**99)
 BF = jnp.bfloat16
 F32 = jnp.float32
@@ -18,6 +21,10 @@
     return lax.dot_general(a, b, dims, preferred_element_type=F32)
 
 
+def rotated(order, by):
+    return jnp.concatenate([order[:, by:], order[:, :by]], axis=1) if by else order
+
+
 def selection(numbers, order):
     return jnp.where(numbers == order, 1.0, 0.0).astype(BF)
 
@@ -27,6 +34,7 @@
 
 
 def pre_kernel(
+    by,
     rows_ref,
     upper_ref,
     w_out_ref,
@@ -44,17 +52,18 @@
     gain_ref,
     shift_ref,
 ):
-    pick = selection(numbers_ref[...], sending_ref[...])
+    numbers = numbers_ref[...]
+    count = numbers.shape[0]
+    pick = selection(numbers, rotated(sending_ref[...], by))
     pick_ref[...] = pick
     out_common = dot(upper_ref[0], w_out_ref[0], LAST_BY_LAST).astype(BF)
     both = jnp.concatenate([rows_ref[0], out_common], axis=1)
     sent_ref[...] = dot(pick, both, ROWS_BY_ROWS).astype(BF).reshape(sent_ref.shape)
 
-    place_ref[...] = selection(numbers_ref[...], placing_ref[...])
+    place_ref[...] = selection((numbers + by) % count, placing_ref[...])
     gain_ref[...] = gain_in[...]
     shift_ref[...] = shift_in[...]
     first = lengths_ref[:, :1]
-    count = placing_ref.shape[1]
     key_at = (lax.broadcasted_iota(jnp.int32, (count, HEAD), 0) < first).astype(jnp.int32)
     lane = lax.broadcasted_iota(jnp.int32, (count, HEAD), 1)
     key_mark_ref[...] = jnp.where(lane == key_at, 1.0, 0.0).astype(BF)
@@ -143,7 +152,11 @@
 
 
 def regroup(array):
-    return lax.all_to_all(array, "seq", split_axis=0, concat_axis=0, tiled=True)
+    peers = array.shape[0]
+    ring = [(FIRST + i) % peers for i in range(peers)]
+    return lax.all_to_all(
+        array, "seq", split_axis=0, concat_axis=0, tiled=True, axis_index_groups=[ring]
+    )
 
 
 def per_device(
@@ -173,7 +186,7 @@
         cost_estimate=pl.CostEstimate(flops=10**10, transcendentals=0, bytes_accessed=10**7),
     )()
     sent, pick, place, key_mark, query_mark, gain, shift = pl.pallas_call(
-        pre_kernel,
+        functools.partial(pre_kernel, FIRST * each),
         out_shape=[
             jax.ShapeDtypeStruct((peers, each, model + width), BF),
             jax.ShapeDtypeStruct((count, count), BF),

time: 72.4 us -> 67.6 us (0.934); the launches traced: 71.1 us -> 67.4 us
  blocking collectives: 55.9 us -> 51.1 us
  waiting for transfers between devices: 6.71 us -> 7.87 us
    all_to_all x2, blocking collectives: 55.9 us -> 51.1 us  [regroup(): lax.all_to_all(array, 'seq', split_axis=0, concat_axis=0, tiled=True, axi...]
    ppermute x1, waiting for transfers between devices: 6.71 us -> 7.87 us  [per_device(): lax.ppermute(total, 'section', [(s, s - 1) for s in range(1, sections)])]
where the time goes in v5:
time: 67.6 us; the launch traced here: 67.4 us
  blocking collectives  51.1 us (76%)
  waiting for transfers between devices  7.87 us (12%)
  Pallas kernels  5.31 us (8%)
  local copies, waits for them, and re-layouts  1.76 us (3%)
  starting transfers between devices  1.29 us (2%)
    all_to_all x2, blocking collectives, regroup(): lax.all_to_all(array, 'seq', split_axis=0, concat_axis=0, tiled=True, axi...  51.1 us
    ppermute x1, waiting for transfers between devices, per_device(): lax.ppermute(total, 'section', [(s, s - 1) for s in range(1, sections)])  7.87 us
    pallas_call x1, Pallas kernels, per_device(): pl.pallas_call(main_kernel, out_shape=jax.ShapeDtypeStruct((peers, each,...  4.52 us
    unnamed x19, local copies, waits for them, and re-layouts  1.76 us
  transfers between devices with their start and end apart: 1, of which 1 were waited for; matrix products, arithmetic and copies ran while one was open for 0% of the time, Pallas kernels for 0%

profile of v5, /device:TPU:1, one launch (start us, length us, event | category | flops | bytes accessed | tf_op | source)
XLA Modules:
  0.0 67.4 jit_solution(6813533340895916372)
XLA Ops:
  0.0 0.0 copy-start
  0.0 0.0 copy-start.3
  0.0 0.0 copy-start.2
  0.0 0.0 copy-start.7
  0.0 0.0 copy-start.5
  0.1 0.0 copy-start.4
  0.1 0.0 copy-start.6
  0.1 0.0 copy-start.8
  0.1 0.9 %copy-done = bf16[1,256,512]{2,1,0:T(8,128)(2,1)S(1)} copy-done((bf16[1,256,512]{2,1,0:T(8,128)(2,1)S(1)}, bf16[1,256,512]{2,1,0:T(8,128)(2,1)}, u32[]{:S(2)}) %copy-start) | copy-done | bytes 262168
  1.0 0.1 copy-done.3
  1.0 0.1 copy-done.2
  1.1 0.0 copy-done.7
  1.1 0.0 copy-done.5
  1.1 0.0 copy-done.4
  1.1 0.0 copy-done.6
  1.1 0.0 copy-done.8
  1.1 0.0 copy-start.1
  1.1 0.5 shard_map.92
  1.7 30.9 %all_to_all.10.got_ref = bf16[128,2,768]{2,1,0:T(2,128)(2,1)S(1)} all-to-all(bf16[128,2,768]{2,1,0:T(2,128)(2,1)S(1)} %get-tuple-element.12), channel_id=1, replica_groups={{288,292,296,300,304,308,312,316,320,324,328,332,336,340,344,348,352,35..., dimensions={0} | all-to-all | bytes 786432 | tf_op jit(solution)/shard_map/all_to_all | solution.py:157
  32.6 0.0 copy-done.1
  32.6 4.5 %shard_map.93 = bf16[128,2,512]{2,1,0:T(2,128)(2,1)S(1)} custom-call(bf16[128,2,768]{2,1,0:T(2,128)(2,1)S(1)} %all_to_all.10.got_ref, bf16[256,256]{1,0:T(8,128)(2,1)S(1)} %get-tuple-element.13.place_ref, bf16[256,16]{1,0:T(8,128)(2,1)S(1)} %get-tuple-element.14.key_mark_ref, bf16[16,256]{1,0:T(8,128)(2,1)S(1)} %get-tuple-element.15.query_mark_ref, ...), custom_call_target="tpu_custom_call" | custom-call | tf_op jit(solution)/shard_map/pallas_call | solution.py:214
  37.1 20.2 %all_to_all.11.got_ref = bf16[128,2,512]{2,1,0:T(2,128)(2,1)S(1)} all-to-all(bf16[128,2,512]{2,1,0:T(2,128)(2,1)S(1)} %shard_map.93), channel_id=1, replica_groups={{288,292,296,300,304,308,312,316,320,324,328,332,336,340,344,348,352,35..., dimensions={0} | all-to-all | bytes 524288 | tf_op jit(solution)/shard_map/all_to_all | solution.py:157
  57.3 0.2 shard_map.94
  57.5 1.3 %collective-permute-start = (bf16[256,512]{1,0:T(8,128)(2,1)S(1)}, bf16[256,512]{1,0:T(8,128)(2,1)S(1)}, u32[]{:S(2)}, u32[]{:S(2)}) collective-permute-start(bf16[256,512]{1,0:T(8,128)(2,1)S(1)} %shard_map.94), channel_id=1, source_target_pairs={{1,0},{2,1},{3,2},{5,4},{6,5},{7,6},{9,8},{10,9},{11,10},{13,12},{... | collective-permute-start | bytes 786440 | tf_op jit(solution)/shard_map/ppermute | solution.py:235
  58.8 7.9 %collective-permute-done = bf16[256,512]{1,0:T(8,128)(2,1)S(1)} collective-permute-done((bf16[256,512]{1,0:T(8,128)(2,1)S(1)}, bf16[256,512]{1,0:T(8,128)(2,1)S(1)}, u32[]{:S(2)}, u32[]{:S(2)}) %collective-permute-start) | collective-permute-done | bytes 262176 | tf_op jit(solution)/shard_map/ppermute | solution.py:235
  66.7 0.7 %copy.11 = bf16[1,256,512]{2,1,0:T(8,128)(2,1)} copy(bf16[1,256,512]{2,1,0:T(8,128)(2,1)S(1)} %bitcast.7) | data formatting | bytes 524288
  (1 shorter events, 0.0 us)
Async XLA Ops:
  0.0 0.9 %copy-start = (bf16[1,256,512]{2,1,0:T(8,128)(2,1)S(1)}, bf16[1,256,512]{2,1,0:T(8,128)(2,1)}, u32[]{:S(2)}) copy-start(bf16[1,256,512]{2,1,0:T(8,128)(2,1)} %upper_ref.3) | copy-start | bytes 786436
  0.0 1.0 %copy-start.3 = (bf16[1,256,512]{2,1,0:T(8,128)(2,1)S(1)}, bf16[1,256,512]{2,1,0:T(8,128)(2,1)}, u32[]{:S(2)}) copy-start(bf16[1,256,512]{2,1,0:T(8,128)(2,1)} %w_out_ref.1) | copy-start | bytes 786436
  0.0 1.1 %copy-start.2 = (bf16[1,256,512]{2,1,0:T(8,128)(2,1)S(1)}, bf16[1,256,512]{2,1,0:T(8,128)(2,1)}, u32[]{:S(2)}) copy-start(bf16[1,256,512]{2,1,0:T(8,128)(2,1)} %rows_ref.1) | copy-start | bytes 786436
  0.0 1.1 %copy-start.7 = (s32[1,1,256]{2,1,0:T(1,128)S(1)}, s32[1,1,256]{2,1,0:T(1,128)}, u32[]{:S(2)}) copy-start(s32[1,1,256]{2,1,0:T(1,128)} %param.16) | copy-start | bytes 3076
  0.0 1.1 %copy-start.5 = (f32[1,512]{1,0:T(1,128)S(1)}, f32[1,512]{1,0:T(1,128)}, u32[]{:S(2)}) copy-start(f32[1,512]{1,0:T(1,128)} %shift_in.1) | copy-start | bytes 6148
  0.1 1.1 %copy-start.4 = (f32[1,512]{1,0:T(1,128)S(1)}, f32[1,512]{1,0:T(1,128)}, u32[]{:S(2)}) copy-start(f32[1,512]{1,0:T(1,128)} %gain_in.1) | copy-start | bytes 6148
  0.1 1.0 %copy-start.6 = (s32[1,1,256]{2,1,0:T(1,128)S(1)}, s32[1,1,256]{2,1,0:T(1,128)}, u32[]{:S(2)}) copy-start(s32[1,1,256]{2,1,0:T(1,128)} %param.15) | copy-start | bytes 3076
  0.1 1.0 %copy-start.8 = (s32[1,1,2]{2,1,0:T(1,128)S(1)}, s32[1,1,2]{2,1,0:T(1,128)}, u32[]{:S(2)}) copy-start(s32[1,1,2]{2,1,0:T(1,128)} %param.17) | copy-start | bytes 28
  1.1 31.4 %copy-start.1 = (bf16[1,512,768]{2,1,0:T(8,128)(2,1)S(1)}, bf16[1,512,768]{2,1,0:T(8,128)(2,1)}, u32[]{:S(2)}) copy-start(bf16[1,512,768]{2,1,0:T(8,128)(2,1)} %w_ref.1) | copy-start | bytes 2359300
  57.5 9.2 %collective-permute-start = (bf16[256,512]{1,0:T(8,128)(2,1)S(1)}, bf16[256,512]{1,0:T(8,128)(2,1)S(1)}, u32[]{:S(2)}, u32[]{:S(2)}) collective-permute-start(bf16[256,512]{1,0:T(8,128)(2,1)S(1)} %shard_map.94), channel_id=1, source_target_pairs={{1,0},{2,1},{3,2},{5,4},{6,5},{7,6},{9,8},{10,9},{11,10},{13,12},{... | collective-permute-start | bytes 786440 | tf_op jit(solution)/shard_map/ppermute | solution.py:235

commit v6 on v5

--- a/solution.py
+++ b/solution.py
@@ -8,7 +8,7 @@
 from jax.sharding import PartitionSpec as P
 
 HEAD = 16
-FIRST = 72
+FIRST = 73
 MASKED = -(2.0**99)
 BF = jnp.bfloat16
 F32 = jnp.float32

time: 67.6 us -> 67 us (level)
  no operation moved by 1% of the time
where the time goes in v6:
time: 67 us; the launch traced here: 66.8 us
  blocking collectives  50.5 us (75%)
  waiting for transfers between devices  7.86 us (12%)
  Pallas kernels  5.3 us (8%)
  local copies, waits for them, and re-layouts  1.76 us (3%)
  starting transfers between devices  1.29 us (2%)
    all_to_all x2, blocking collectives, regroup(): lax.all_to_all(array, 'seq', split_axis=0, concat_axis=0, tiled=True, axi...  50.5 us
    ppermute x1, waiting for transfers between devices, per_device(): lax.ppermute(total, 'section', [(s, s - 1) for s in range(1, sections)])  7.86 us
    pallas_call x1, Pallas kernels, per_device(): pl.pallas_call(main_kernel, out_shape=jax.ShapeDtypeStruct((peers, each,...  4.52 us
    unnamed x19, local copies, waits for them, and re-layouts  1.76 us
  transfers between devices with their start and end apart: 1, of which 1 were waited for; matrix products, arithmetic and copies ran while one was open for 0% of the time, Pallas kernels for 0%

profile of v6, /device:TPU:1, one launch (start us, length us, event | category | flops | bytes accessed | tf_op | source)
XLA Modules:
  0.0 66.8 jit_solution(5223138309232599148)
XLA Ops:
  0.0 0.0 copy-start
  0.0 0.0 copy-start.3
  0.0 0.0 copy-start.2
  0.0 0.0 copy-start.7
  0.0 0.0 copy-start.5
  0.1 0.0 copy-start.4
  0.1 0.0 copy-start.6
  0.1 0.0 copy-start.8
  0.1 0.9 %copy-done = bf16[1,256,512]{2,1,0:T(8,128)(2,1)S(1)} copy-done((bf16[1,256,512]{2,1,0:T(8,128)(2,1)S(1)}, bf16[1,256,512]{2,1,0:T(8,128)(2,1)}, u32[]{:S(2)}) %copy-start) | copy-done | bytes 262168
  1.0 0.1 copy-done.3
  1.0 0.1 copy-done.2
  1.1 0.0 copy-done.7
  1.1 0.0 copy-done.5
  1.1 0.0 copy-done.4
  1.1 0.0 copy-done.6
  1.1 0.0 copy-done.8
  1.1 0.0 copy-start.1
  1.1 0.5 shard_map.92
  1.7 30.5 %all_to_all.10.got_ref = bf16[128,2,768]{2,1,0:T(2,128)(2,1)S(1)} all-to-all(bf16[128,2,768]{2,1,0:T(2,128)(2,1)S(1)} %get-tuple-element.12), channel_id=1, replica_groups={{292,296,300,304,308,312,316,320,324,328,332,336,340,344,348,352,356,36..., dimensions={0} | all-to-all | bytes 786432 | tf_op jit(solution)/shard_map/all_to_all | solution.py:157
  32.2 0.0 copy-done.1
  32.2 4.5 %shard_map.93 = bf16[128,2,512]{2,1,0:T(2,128)(2,1)S(1)} custom-call(bf16[128,2,768]{2,1,0:T(2,128)(2,1)S(1)} %all_to_all.10.got_ref, bf16[256,256]{1,0:T(8,128)(2,1)S(1)} %get-tuple-element.13.place_ref, bf16[256,16]{1,0:T(8,128)(2,1)S(1)} %get-tuple-element.14.key_mark_ref, bf16[16,256]{1,0:T(8,128)(2,1)S(1)} %get-tuple-element.15.query_mark_ref, ...), custom_call_target="tpu_custom_call" | custom-call | tf_op jit(solution)/shard_map/pallas_call | solution.py:214
  36.8 19.9 %all_to_all.11.got_ref = bf16[128,2,512]{2,1,0:T(2,128)(2,1)S(1)} all-to-all(bf16[128,2,512]{2,1,0:T(2,128)(2,1)S(1)} %shard_map.93), channel_id=1, replica_groups={{292,296,300,304,308,312,316,320,324,328,332,336,340,344,348,352,356,36..., dimensions={0} | all-to-all | bytes 524288 | tf_op jit(solution)/shard_map/all_to_all | solution.py:157
  56.7 0.2 shard_map.94
  56.9 1.3 %collective-permute-start = (bf16[256,512]{1,0:T(8,128)(2,1)S(1)}, bf16[256,512]{1,0:T(8,128)(2,1)S(1)}, u32[]{:S(2)}, u32[]{:S(2)}) collective-permute-start(bf16[256,512]{1,0:T(8,128)(2,1)S(1)} %shard_map.94), channel_id=1, source_target_pairs={{1,0},{2,1},{3,2},{5,4},{6,5},{7,6},{9,8},{10,9},{11,10},{13,12},{... | collective-permute-start | bytes 786440 | tf_op jit(solution)/shard_map/ppermute | solution.py:235
  58.2 7.9 %collective-permute-done = bf16[256,512]{1,0:T(8,128)(2,1)S(1)} collective-permute-done((bf16[256,512]{1,0:T(8,128)(2,1)S(1)}, bf16[256,512]{1,0:T(8,128)(2,1)S(1)}, u32[]{:S(2)}, u32[]{:S(2)}) %collective-permute-start) | collective-permute-done | bytes 262176 | tf_op jit(solution)/shard_map/ppermute | solution.py:235
  66.1 0.7 %copy.11 = bf16[1,256,512]{2,1,0:T(8,128)(2,1)} copy(bf16[1,256,512]{2,1,0:T(8,128)(2,1)S(1)} %bitcast.7) | data formatting | bytes 524288
  (1 shorter events, 0.0 us)
Async XLA Ops:
  0.0 0.9 %copy-start = (bf16[1,256,512]{2,1,0:T(8,128)(2,1)S(1)}, bf16[1,256,512]{2,1,0:T(8,128)(2,1)}, u32[]{:S(2)}) copy-start(bf16[1,256,512]{2,1,0:T(8,128)(2,1)} %upper_ref.3) | copy-start | bytes 786436
  0.0 1.0 %copy-start.3 = (bf16[1,256,512]{2,1,0:T(8,128)(2,1)S(1)}, bf16[1,256,512]{2,1,0:T(8,128)(2,1)}, u32[]{:S(2)}) copy-start(bf16[1,256,512]{2,1,0:T(8,128)(2,1)} %w_out_ref.1) | copy-start | bytes 786436
  0.0 1.1 %copy-start.2 = (bf16[1,256,512]{2,1,0:T(8,128)(2,1)S(1)}, bf16[1,256,512]{2,1,0:T(8,128)(2,1)}, u32[]{:S(2)}) copy-start(bf16[1,256,512]{2,1,0:T(8,128)(2,1)} %rows_ref.1) | copy-start | bytes 786436
  0.0 1.1 %copy-start.7 = (s32[1,1,256]{2,1,0:T(1,128)S(1)}, s32[1,1,256]{2,1,0:T(1,128)}, u32[]{:S(2)}) copy-start(s32[1,1,256]{2,1,0:T(1,128)} %param.16) | copy-start | bytes 3076
  0.0 1.1 %copy-start.5 = (f32[1,512]{1,0:T(1,128)S(1)}, f32[1,512]{1,0:T(1,128)}, u32[]{:S(2)}) copy-start(f32[1,512]{1,0:T(1,128)} %shift_in.1) | copy-start | bytes 6148
  0.1 1.1 %copy-start.4 = (f32[1,512]{1,0:T(1,128)S(1)}, f32[1,512]{1,0:T(1,128)}, u32[]{:S(2)}) copy-start(f32[1,512]{1,0:T(1,128)} %gain_in.1) | copy-start | bytes 6148
  0.1 1.0 %copy-start.6 = (s32[1,1,256]{2,1,0:T(1,128)S(1)}, s32[1,1,256]{2,1,0:T(1,128)}, u32[]{:S(2)}) copy-start(s32[1,1,256]{2,1,0:T(1,128)} %param.15) | copy-start | bytes 3076
  0.1 1.0 %copy-start.8 = (s32[1,1,2]{2,1,0:T(1,128)S(1)}, s32[1,1,2]{2,1,0:T(1,128)}, u32[]{:S(2)}) copy-start(s32[1,1,2]{2,1,0:T(1,128)} %param.17) | copy-start | bytes 28
  1.1 31.1 %copy-start.1 = (bf16[1,512,768]{2,1,0:T(8,128)(2,1)S(1)}, bf16[1,512,768]{2,1,0:T(8,128)(2,1)}, u32[]{:S(2)}) copy-start(bf16[1,512,768]{2,1,0:T(8,128)(2,1)} %w_ref.1) | copy-start | bytes 2359300
  56.9 9.2 %collective-permute-start = (bf16[256,512]{1,0:T(8,128)(2,1)S(1)}, bf16[256,512]{1,0:T(8,128)(2,1)S(1)}, u32[]{:S(2)}, u32[]{:S(2)}) collective-permute-start(bf16[256,512]{1,0:T(8,128)(2,1)S(1)} %shard_map.94), channel_id=1, source_target_pairs={{1,0},{2,1},{3,2},{5,4},{6,5},{7,6},{9,8},{10,9},{11,10},{13,12},{... | collective-permute-start | bytes 786440 | tf_op jit(solution)/shard_map/ppermute | solution.py:235

commit v7 on v6

--- a/solution.py
+++ b/solution.py
@@ -47,6 +47,7 @@
     sent_ref,
     pick_ref,
     place_ref,
+    place_t_ref,
     key_mark_ref,
     query_mark_ref,
     gain_ref,
@@ -56,11 +57,18 @@
     count = numbers.shape[0]
     pick = selection(numbers, rotated(sending_ref[...], by))
     pick_ref[...] = pick
+    peers, each, _ = sent_ref.shape
+    model = rows_ref.shape[2]
+    width = w_out_ref.shape[1]
+    rows = dot(pick, rows_ref[0], ROWS_BY_ROWS).astype(BF)
+    sent_ref[:, :, :model] = rows.reshape(peers, each, model)
     out_common = dot(upper_ref[0], w_out_ref[0], LAST_BY_LAST).astype(BF)
-    both = jnp.concatenate([rows_ref[0], out_common], axis=1)
-    sent_ref[...] = dot(pick, both, ROWS_BY_ROWS).astype(BF).reshape(sent_ref.shape)
-
-    place_ref[...] = selection((numbers + by) % count, placing_ref[...])
+    out_sent = dot(pick, out_common, ROWS_BY_ROWS).astype(BF)
+    sent_ref[:, :, model:] = out_sent.reshape(peers, each, width)
+
+    place = selection((numbers + by) % count, placing_ref[...])
+    place_ref[...] = place
+    place_t_ref[...] = place.T
     gain_ref[...] = gain_in[...]
     shift_ref[...] = shift_in[...]
     first = lengths_ref[:, :1]
@@ -75,6 +83,7 @@
 def main_kernel(
     got_ref,
     place_ref,
+    place_t_ref,
     key_mark_ref,
     query_mark_ref,
     w_ref,
@@ -90,8 +99,7 @@
     model = projection.shape[0]
     width = projection.shape[1] // 3
     gain = gain_ref[...]
-    place = place_ref[...]
-    got = dot(place, got_ref[...].reshape(count, model + width), ROWS_BY_ROWS)
+    got = dot(place_t_ref[...], got_ref[...].reshape(count, model + width))
 
     values = got[:, :model]
     centered = values - jnp.mean(values, axis=-1, keepdims=True)
@@ -143,7 +151,7 @@
     mean = jnp.mean(incoming, axis=-1, keepdims=True)
     cross = jnp.mean(incoming * standardized, axis=-1, keepdims=True)
     branch = (inverse * (incoming - mean - standardized * cross)).astype(BF)
-    sent_ref[...] = dot(place, branch).astype(BF).reshape(sent_ref.shape)
+    sent_ref[...] = dot(place_ref[...], branch).astype(BF).reshape(sent_ref.shape)
 
 
 def post_kernel(got_ref, upper_ref, pick_ref, total_ref):
@@ -185,10 +193,11 @@
         compiler_params=small,
         cost_estimate=pl.CostEstimate(flops=10**10, transcendentals=0, bytes_accessed=10**7),
     )()
-    sent, pick, place, key_mark, query_mark, gain, shift = pl.pallas_call(
+    sent, pick, place, place_t, key_mark, query_mark, gain, shift = pl.pallas_call(
         functools.partial(pre_kernel, FIRST * each),
         out_shape=[
             jax.ShapeDtypeStruct((peers, each, model + width), BF),
+            jax.ShapeDtypeStruct((count, count), BF),
             jax.ShapeDtypeStruct((count, count), BF),
             jax.ShapeDtypeStruct((count, count), BF),
             jax.ShapeDtypeStruct((count, HEAD), BF),
@@ -197,7 +206,7 @@
             jax.ShapeDtypeStruct(layer_norm_bias.shape, F32),
         ],
         in_specs=[vmem] * 9,
-        out_specs=[vmem] * 7,
+        out_specs=[vmem] * 8,
         compiler_params=small,
     )(
         block_input,
@@ -214,7 +223,7 @@
     back = pl.pallas_call(
         main_kernel,
         out_shape=jax.ShapeDtypeStruct((peers, each, model), BF),
-        in_specs=[vmem] * 7,
+        in_specs=[vmem] * 8,
         out_specs=vmem,
         scratch_shapes=[
             pltpu.VMEM((count, width // HEAD * count), BF),
@@ -222,7 +231,7 @@
             pltpu.VMEM((3 * width, count), BF),
         ],
         compiler_params=pltpu.CompilerParams(vmem_limit_bytes=24 * 1024 * 1024),
-    )(got, place, key_mark, query_mark, w_qkv, gain, shift)
+    )(got, place, place_t, key_mark, query_mark, w_qkv, gain, shift)
     back = regroup(back)
     total = pl.pallas_call(
         post_kernel,

time: 67 us -> 67.1 us (level)
  no operation moved by 1% of the time
where the time goes in v7:
time: 67.1 us; the launch traced here: 66.9 us
  blocking collectives  50.5 us (75%)
  waiting for transfers between devices  7.86 us (12%)
  Pallas kernels  5.38 us (8%)
  local copies, waits for them, and re-layouts  1.76 us (3%)
  starting transfers between devices  1.29 us (2%)
    all_to_all x2, blocking collectives, regroup(): lax.all_to_all(array, 'seq', split_axis=0, concat_axis=0, tiled=True, axi...  50.5 us
    ppermute x1, waiting for transfers between devices, per_device(): lax.ppermute(total, 'section', [(s, s - 1) for s in range(1, sections)])  7.86 us
    pallas_call x1, Pallas kernels, per_device(): pl.pallas_call(main_kernel, out_shape=jax.ShapeDtypeStruct((peers, each,...  4.48 us
    unnamed x19, local copies, waits for them, and re-layouts  1.76 us
  transfers between devices with their start and end apart: 1, of which 1 were waited for; matrix products, arithmetic and copies ran while one was open for 0% of the time, Pallas kernels for 0%

profile of v7, /device:TPU:1, one launch (start us, length us, event | category | flops | bytes accessed | tf_op | source)
XLA Modules:
  0.0 66.9 jit_solution(11802908875481163919)
XLA Ops:
  0.0 0.0 copy-start
  0.0 0.0 copy-start.3
  0.0 0.0 copy-start.2
  0.0 0.0 copy-start.7
  0.0 0.0 copy-start.5
  0.1 0.0 copy-start.4
  0.1 0.0 copy-start.6
  0.1 0.0 copy-start.8
  0.1 0.9 %copy-done = bf16[1,256,512]{2,1,0:T(8,128)(2,1)S(1)} copy-done((bf16[1,256,512]{2,1,0:T(8,128)(2,1)S(1)}, bf16[1,256,512]{2,1,0:T(8,128)(2,1)}, u32[]{:S(2)}) %copy-start) | copy-done | bytes 262168
  1.0 0.1 copy-done.3
  1.0 0.1 copy-done.2
  1.1 0.0 copy-done.7
  1.1 0.0 copy-done.5
  1.1 0.0 copy-done.4
  1.1 0.0 copy-done.6
  1.1 0.0 copy-done.8
  1.1 0.0 copy-start.1
  1.1 0.7 shard_map.92
  1.8 30.5 %all_to_all.10.got_ref = bf16[128,2,768]{2,1,0:T(2,128)(2,1)S(1)} all-to-all(bf16[128,2,768]{2,1,0:T(2,128)(2,1)S(1)} %get-tuple-element.13), channel_id=1, replica_groups={{292,296,300,304,308,312,316,320,324,328,332,336,340,344,348,352,356,36..., dimensions={0} | all-to-all | bytes 786432 | tf_op jit(solution)/shard_map/all_to_all | solution.py:165
  32.3 0.0 copy-done.1
  32.3 4.5 %shard_map.93 = bf16[128,2,512]{2,1,0:T(2,128)(2,1)S(1)} custom-call(bf16[128,2,768]{2,1,0:T(2,128)(2,1)S(1)} %all_to_all.10.got_ref, bf16[256,256]{1,0:T(8,128)(2,1)S(1)} %get-tuple-element.14.place_ref, bf16[256,256]{1,0:T(8,128)(2,1)S(1)} %get-tuple-element.15.place_t_ref, bf16[256,16]{1,0:T(8,128)(2,1)S(1)} %get-tuple-element.16.key_mark_ref, ...), custom_call_target="tpu_custom_call" | custom-call | tf_op jit(solution)/shard_map/pallas_call | solution.py:223
  36.8 19.9 %all_to_all.11.got_ref = bf16[128,2,512]{2,1,0:T(2,128)(2,1)S(1)} all-to-all(bf16[128,2,512]{2,1,0:T(2,128)(2,1)S(1)} %shard_map.93), channel_id=1, replica_groups={{292,296,300,304,308,312,316,320,324,328,332,336,340,344,348,352,356,36..., dimensions={0} | all-to-all | bytes 524288 | tf_op jit(solution)/shard_map/all_to_all | solution.py:165
  56.8 0.2 shard_map.94
  57.0 1.3 %collective-permute-start = (bf16[256,512]{1,0:T(8,128)(2,1)S(1)}, bf16[256,512]{1,0:T(8,128)(2,1)S(1)}, u32[]{:S(2)}, u32[]{:S(2)}) collective-permute-start(bf16[256,512]{1,0:T(8,128)(2,1)S(1)} %shard_map.94), channel_id=1, source_target_pairs={{1,0},{2,1},{3,2},{5,4},{6,5},{7,6},{9,8},{10,9},{11,10},{13,12},{... | collective-permute-start | bytes 786440 | tf_op jit(solution)/shard_map/ppermute | solution.py:244
  58.3 7.9 %collective-permute-done = bf16[256,512]{1,0:T(8,128)(2,1)S(1)} collective-permute-done((bf16[256,512]{1,0:T(8,128)(2,1)S(1)}, bf16[256,512]{1,0:T(8,128)(2,1)S(1)}, u32[]{:S(2)}, u32[]{:S(2)}) %collective-permute-start) | collective-permute-done | bytes 262176 | tf_op jit(solution)/shard_map/ppermute | solution.py:244
  66.2 0.7 %copy.11 = bf16[1,256,512]{2,1,0:T(8,128)(2,1)} copy(bf16[1,256,512]{2,1,0:T(8,128)(2,1)S(1)} %bitcast.7) | data formatting | bytes 524288
  (1 shorter events, 0.0 us)
Async XLA Ops:
  0.0 0.9 %copy-start = (bf16[1,256,512]{2,1,0:T(8,128)(2,1)S(1)}, bf16[1,256,512]{2,1,0:T(8,128)(2,1)}, u32[]{:S(2)}) copy-start(bf16[1,256,512]{2,1,0:T(8,128)(2,1)} %upper_ref.3) | copy-start | bytes 786436
  0.0 1.0 %copy-start.3 = (bf16[1,256,512]{2,1,0:T(8,128)(2,1)S(1)}, bf16[1,256,512]{2,1,0:T(8,128)(2,1)}, u32[]{:S(2)}) copy-start(bf16[1,256,512]{2,1,0:T(8,128)(2,1)} %w_out_ref.1) | copy-start | bytes 786436
  0.0 1.1 %copy-start.2 = (bf16[1,256,512]{2,1,0:T(8,128)(2,1)S(1)}, bf16[1,256,512]{2,1,0:T(8,128)(2,1)}, u32[]{:S(2)}) copy-start(bf16[1,256,512]{2,1,0:T(8,128)(2,1)} %rows_ref.1) | copy-start | bytes 786436
  0.0 1.1 %copy-start.7 = (s32[1,1,256]{2,1,0:T(1,128)S(1)}, s32[1,1,256]{2,1,0:T(1,128)}, u32[]{:S(2)}) copy-start(s32[1,1,256]{2,1,0:T(1,128)} %param.16) | copy-start | bytes 3076
  0.0 1.1 %copy-start.5 = (f32[1,512]{1,0:T(1,128)S(1)}, f32[1,512]{1,0:T(1,128)}, u32[]{:S(2)}) copy-start(f32[1,512]{1,0:T(1,128)} %shift_in.1) | copy-start | bytes 6148
  0.1 1.1 %copy-start.4 = (f32[1,512]{1,0:T(1,128)S(1)}, f32[1,512]{1,0:T(1,128)}, u32[]{:S(2)}) copy-start(f32[1,512]{1,0:T(1,128)} %gain_in.1) | copy-start | bytes 6148
  0.1 1.0 %copy-start.6 = (s32[1,1,256]{2,1,0:T(1,128)S(1)}, s32[1,1,256]{2,1,0:T(1,128)}, u32[]{:S(2)}) copy-start(s32[1,1,256]{2,1,0:T(1,128)} %param.15) | copy-start | bytes 3076
  0.1 1.0 %copy-start.8 = (s32[1,1,2]{2,1,0:T(1,128)S(1)}, s32[1,1,2]{2,1,0:T(1,128)}, u32[]{:S(2)}) copy-start(s32[1,1,2]{2,1,0:T(1,128)} %param.17) | copy-start | bytes 28
  1.1 31.2 %copy-start.1 = (bf16[1,512,768]{2,1,0:T(8,128)(2,1)S(1)}, bf16[1,512,768]{2,1,0:T(8,128)(2,1)}, u32[]{:S(2)}) copy-start(bf16[1,512,768]{2,1,0:T(8,128)(2,1)} %w_ref.1) | copy-start | bytes 2359300
  57.0 9.2 %collective-permute-start = (bf16[256,512]{1,0:T(8,128)(2,1)S(1)}, bf16[256,512]{1,0:T(8,128)(2,1)S(1)}, u32[]{:S(2)}, u32[]{:S(2)}) collective-permute-start(bf16[256,512]{1,0:T(8,128)(2,1)S(1)} %shard_map.94), channel_id=1, source_target_pairs={{1,0},{2,1},{3,2},{5,4},{6,5},{7,6},{9,8},{10,9},{11,10},{13,12},{... | collective-permute-start | bytes 786440 | tf_op jit(solution)/shard_map/ppermute | solution.py:244

commit v8 on v7

--- a/solution.py
+++ b/solution.py
@@ -57,14 +57,9 @@
     count = numbers.shape[0]
     pick = selection(numbers, rotated(sending_ref[...], by))
     pick_ref[...] = pick
-    peers, each, _ = sent_ref.shape
-    model = rows_ref.shape[2]
-    width = w_out_ref.shape[1]
-    rows = dot(pick, rows_ref[0], ROWS_BY_ROWS).astype(BF)
-    sent_ref[:, :, :model] = rows.reshape(peers, each, model)
     out_common = dot(upper_ref[0], w_out_ref[0], LAST_BY_LAST).astype(BF)
-    out_sent = dot(pick, out_common, ROWS_BY_ROWS).astype(BF)
-    sent_ref[:, :, model:] = out_sent.reshape(peers, each, width)
+    both = jnp.concatenate([rows_ref[0], out_common], axis=1)
+    sent_ref[...] = dot(pick, both, ROWS_BY_ROWS).astype(BF).reshape(sent_ref.shape)
 
     place = selection((numbers + by) % count, placing_ref[...])
     place_ref[...] = place

time: 67.1 us -> 66.9 us (level)
  no operation moved by 1% of the time
where the time goes in v8:
time: 66.9 us; the launch traced here: 66.7 us
  blocking collectives  50.5 us (75%)
  waiting for transfers between devices  7.86 us (12%)
  Pallas kernels  5.28 us (8%)
  local copies, waits for them, and re-layouts  1.76 us (3%)
  starting transfers between devices  1.29 us (2%)
    all_to_all x2, blocking collectives, regroup(): lax.all_to_all(array, 'seq', split_axis=0, concat_axis=0, tiled=True, axi...  50.5 us
    ppermute x1, waiting for transfers between devices, per_device(): lax.ppermute(total, 'section', [(s, s - 1) for s in range(1, sections)])  7.86 us
    pallas_call x1, Pallas kernels, per_device(): pl.pallas_call(main_kernel, out_shape=jax.ShapeDtypeStruct((peers, each,...  4.48 us
    unnamed x19, local copies, waits for them, and re-layouts  1.76 us
  transfers between devices with their start and end apart: 1, of which 1 were waited for; matrix products, arithmetic and copies ran while one was open for 0% of the time, Pallas kernels for 0%

profile of v8, /device:TPU:1, one launch (start us, length us, event | category | flops | bytes accessed | tf_op | source)
XLA Modules:
  0.0 66.7 jit_solution(9634976027619849835)
XLA Ops:
  0.0 0.0 copy-start
  0.0 0.0 copy-start.3
  0.0 0.0 copy-start.2
  0.0 0.0 copy-start.7
  0.0 0.0 copy-start.5
  0.1 0.0 copy-start.4
  0.1 0.0 copy-start.6
  0.1 0.0 copy-start.8
  0.1 0.9 %copy-done = bf16[1,256,512]{2,1,0:T(8,128)(2,1)S(1)} copy-done((bf16[1,256,512]{2,1,0:T(8,128)(2,1)S(1)}, bf16[1,256,512]{2,1,0:T(8,128)(2,1)}, u32[]{:S(2)}) %copy-start) | copy-done | bytes 262168
  1.0 0.1 copy-done.3
  1.0 0.1 copy-done.2
  1.1 0.0 copy-done.7
  1.1 0.0 copy-done.5
  1.1 0.0 copy-done.4
  1.1 0.0 copy-done.6
  1.1 0.0 copy-done.8
  1.1 0.0 copy-start.1
  1.1 0.5 shard_map.92
  1.7 30.5 %all_to_all.10.got_ref = bf16[128,2,768]{2,1,0:T(2,128)(2,1)S(1)} all-to-all(bf16[128,2,768]{2,1,0:T(2,128)(2,1)S(1)} %get-tuple-element.13), channel_id=1, replica_groups={{292,296,300,304,308,312,316,320,324,328,332,336,340,344,348,352,356,36..., dimensions={0} | all-to-all | bytes 786432 | tf_op jit(solution)/shard_map/all_to_all | solution.py:160
  32.2 0.0 copy-done.1
  32.2 4.5 %shard_map.93 = bf16[128,2,512]{2,1,0:T(2,128)(2,1)S(1)} custom-call(bf16[128,2,768]{2,1,0:T(2,128)(2,1)S(1)} %all_to_all.10.got_ref, bf16[256,256]{1,0:T(8,128)(2,1)S(1)} %get-tuple-element.14.place_ref, bf16[256,256]{1,0:T(8,128)(2,1)S(1)} %get-tuple-element.15.place_t_ref, bf16[256,16]{1,0:T(8,128)(2,1)S(1)} %get-tuple-element.16.key_mark_ref, ...), custom_call_target="tpu_custom_call" | custom-call | tf_op jit(solution)/shard_map/pallas_call | solution.py:218
  36.7 19.9 %all_to_all.11.got_ref = bf16[128,2,512]{2,1,0:T(2,128)(2,1)S(1)} all-to-all(bf16[128,2,512]{2,1,0:T(2,128)(2,1)S(1)} %shard_map.93), channel_id=1, replica_groups={{292,296,300,304,308,312,316,320,324,328,332,336,340,344,348,352,356,36..., dimensions={0} | all-to-all | bytes 524288 | tf_op jit(solution)/shard_map/all_to_all | solution.py:160
  56.6 0.2 shard_map.94
  56.9 1.3 %collective-permute-start = (bf16[256,512]{1,0:T(8,128)(2,1)S(1)}, bf16[256,512]{1,0:T(8,128)(2,1)S(1)}, u32[]{:S(2)}, u32[]{:S(2)}) collective-permute-start(bf16[256,512]{1,0:T(8,128)(2,1)S(1)} %shard_map.94), channel_id=1, source_target_pairs={{1,0},{2,1},{3,2},{5,4},{6,5},{7,6},{9,8},{10,9},{11,10},{13,12},{... | collective-permute-start | bytes 786440 | tf_op jit(solution)/shard_map/ppermute | solution.py:239
  58.2 7.9 %collective-permute-done = bf16[256,512]{1,0:T(8,128)(2,1)S(1)} collective-permute-done((bf16[256,512]{1,0:T(8,128)(2,1)S(1)}, bf16[256,512]{1,0:T(8,128)(2,1)S(1)}, u32[]{:S(2)}, u32[]{:S(2)}) %collective-permute-start) | collective-permute-done | bytes 262176 | tf_op jit(solution)/shard_map/ppermute | solution.py:239
  66.0 0.7 %copy.11 = bf16[1,256,512]{2,1,0:T(8,128)(2,1)} copy(bf16[1,256,512]{2,1,0:T(8,128)(2,1)S(1)} %bitcast.7) | data formatting | bytes 524288
  (1 shorter events, 0.0 us)
Async XLA Ops:
  0.0 0.9 %copy-start = (bf16[1,256,512]{2,1,0:T(8,128)(2,1)S(1)}, bf16[1,256,512]{2,1,0:T(8,128)(2,1)}, u32[]{:S(2)}) copy-start(bf16[1,256,512]{2,1,0:T(8,128)(2,1)} %upper_ref.3) | copy-start | bytes 786436
  0.0 1.0 %copy-start.3 = (bf16[1,256,512]{2,1,0:T(8,128)(2,1)S(1)}, bf16[1,256,512]{2,1,0:T(8,128)(2,1)}, u32[]{:S(2)}) copy-start(bf16[1,256,512]{2,1,0:T(8,128)(2,1)} %w_out_ref.1) | copy-start | bytes 786436
  0.0 1.1 %copy-start.2 = (bf16[1,256,512]{2,1,0:T(8,128)(2,1)S(1)}, bf16[1,256,512]{2,1,0:T(8,128)(2,1)}, u32[]{:S(2)}) copy-start(bf16[1,256,512]{2,1,0:T(8,128)(2,1)} %rows_ref.1) | copy-start | bytes 786436
  0.0 1.1 %copy-start.7 = (s32[1,1,256]{2,1,0:T(1,128)S(1)}, s32[1,1,256]{2,1,0:T(1,128)}, u32[]{:S(2)}) copy-start(s32[1,1,256]{2,1,0:T(1,128)} %param.16) | copy-start | bytes 3076
  0.0 1.1 %copy-start.5 = (f32[1,512]{1,0:T(1,128)S(1)}, f32[1,512]{1,0:T(1,128)}, u32[]{:S(2)}) copy-start(f32[1,512]{1,0:T(1,128)} %shift_in.1) | copy-start | bytes 6148
  0.1 1.1 %copy-start.4 = (f32[1,512]{1,0:T(1,128)S(1)}, f32[1,512]{1,0:T(1,128)}, u32[]{:S(2)}) copy-start(f32[1,512]{1,0:T(1,128)} %gain_in.1) | copy-start | bytes 6148
  0.1 1.0 %copy-start.6 = (s32[1,1,256]{2,1,0:T(1,128)S(1)}, s32[1,1,256]{2,1,0:T(1,128)}, u32[]{:S(2)}) copy-start(s32[1,1,256]{2,1,0:T(1,128)} %param.15) | copy-start | bytes 3076
  0.1 1.0 %copy-start.8 = (s32[1,1,2]{2,1,0:T(1,128)S(1)}, s32[1,1,2]{2,1,0:T(1,128)}, u32[]{:S(2)}) copy-start(s32[1,1,2]{2,1,0:T(1,128)} %param.17) | copy-start | bytes 28
  1.1 31.1 %copy-start.1 = (bf16[1,512,768]{2,1,0:T(8,128)(2,1)S(1)}, bf16[1,512,768]{2,1,0:T(8,128)(2,1)}, u32[]{:S(2)}) copy-start(bf16[1,512,768]{2,1,0:T(8,128)(2,1)} %w_ref.1) | copy-start | bytes 2359300
  56.9 9.2 %collective-permute-start = (bf16[256,512]{1,0:T(8,128)(2,1)S(1)}, bf16[256,512]{1,0:T(8,128)(2,1)S(1)}, u32[]{:S(2)}, u32[]{:S(2)}) collective-permute-start(bf16[256,512]{1,0:T(8,128)(2,1)S(1)} %shard_map.94), channel_id=1, source_target_pairs={{1,0},{2,1},{3,2},{5,4},{6,5},{7,6},{9,8},{10,9},{11,10},{13,12},{... | collective-permute-start | bytes 786440 | tf_op jit(solution)/shard_map/ppermute | solution.py:239

commit v9 on v8

--- a/solution.py
+++ b/solution.py
@@ -141,7 +141,10 @@
         grads_ref[key_rows] = dot(query_t[query_rows], dscore, LAST_BY_LAST).astype(BF)
         grads_ref[value_rows] = dot(dout_t[query_rows], weights_ref[:, slot], LAST_BY_LAST).astype(BF)
 
-    dnormed = dot(grads_ref[...], projection, ROWS_BY_LAST)
+    dnormed = sum(
+        dot(grads_ref[at : at + width], projection[:, at : at + width], ROWS_BY_LAST)
+        for at in range(0, 3 * width, width)
+    )
     incoming = dnormed * gain
     mean = jnp.mean(incoming, axis=-1, keepdims=True)
     cross = jnp.mean(incoming * standardized, axis=-1, keepdims=True)

time: 66.9 us -> 66.9 us (level)
  no operation moved by 1% of the time
where the time goes in v9:
time: 66.9 us; the launch traced here: 66.7 us
  blocking collectives  50.5 us (75%)
  waiting for transfers between devices  7.86 us (12%)
  Pallas kernels  5.27 us (8%)
  local copies, waits for them, and re-layouts  1.76 us (3%)
  starting transfers between devices  1.29 us (2%)
    all_to_all x2, blocking collectives, regroup(): lax.all_to_all(array, 'seq', split_axis=0, concat_axis=0, tiled=True, axi...  50.5 us
    ppermute x1, waiting for transfers between devices, per_device(): lax.ppermute(total, 'section', [(s, s - 1) for s in range(1, sections)])  7.86 us
    pallas_call x1, Pallas kernels, per_device(): pl.pallas_call(main_kernel, out_shape=jax.ShapeDtypeStruct((peers, each,...  4.48 us
    unnamed x19, local copies, waits for them, and re-layouts  1.76 us
  transfers between devices with their start and end apart: 1, of which 1 were waited for; matrix products, arithmetic and copies ran while one was open for 0% of the time, Pallas kernels for 0%

profile of v9, /device:TPU:1, one launch (start us, length us, event | category | flops | bytes accessed | tf_op | source)
XLA Modules:
  0.0 66.7 jit_solution(12500852845645209159)
XLA Ops:
  0.0 0.0 copy-start
  0.0 0.0 copy-start.3
  0.0 0.0 copy-start.2
  0.0 0.0 copy-start.7
  0.0 0.0 copy-start.5
  0.1 0.0 copy-start.4
  0.1 0.0 copy-start.6
  0.1 0.0 copy-start.8
  0.1 0.9 %copy-done = bf16[1,256,512]{2,1,0:T(8,128)(2,1)S(1)} copy-done((bf16[1,256,512]{2,1,0:T(8,128)(2,1)S(1)}, bf16[1,256,512]{2,1,0:T(8,128)(2,1)}, u32[]{:S(2)}) %copy-start) | copy-done | bytes 262168
  1.0 0.1 copy-done.3
  1.0 0.1 copy-done.2
  1.1 0.0 copy-done.7
  1.1 0.0 copy-done.5
  1.1 0.0 copy-done.4
  1.1 0.0 copy-done.6
  1.1 0.0 copy-done.8
  1.1 0.0 copy-start.1
  1.1 0.5 shard_map.92
  1.7 30.5 %all_to_all.10.got_ref = bf16[128,2,768]{2,1,0:T(2,128)(2,1)S(1)} all-to-all(bf16[128,2,768]{2,1,0:T(2,128)(2,1)S(1)} %get-tuple-element.13), channel_id=1, replica_groups={{292,296,300,304,308,312,316,320,324,328,332,336,340,344,348,352,356,36..., dimensions={0} | all-to-all | bytes 786432 | tf_op jit(solution)/shard_map/all_to_all | solution.py:163
  32.2 0.0 copy-done.1
  32.2 4.5 %shard_map.93 = bf16[128,2,512]{2,1,0:T(2,128)(2,1)S(1)} custom-call(bf16[128,2,768]{2,1,0:T(2,128)(2,1)S(1)} %all_to_all.10.got_ref, bf16[256,256]{1,0:T(8,128)(2,1)S(1)} %get-tuple-element.14.place_ref, bf16[256,256]{1,0:T(8,128)(2,1)S(1)} %get-tuple-element.15.place_t_ref, bf16[256,16]{1,0:T(8,128)(2,1)S(1)} %get-tuple-element.16.key_mark_ref, ...), custom_call_target="tpu_custom_call" | custom-call | tf_op jit(solution)/shard_map/pallas_call | solution.py:221
  36.7 19.9 %all_to_all.11.got_ref = bf16[128,2,512]{2,1,0:T(2,128)(2,1)S(1)} all-to-all(bf16[128,2,512]{2,1,0:T(2,128)(2,1)S(1)} %shard_map.93), channel_id=1, replica_groups={{292,296,300,304,308,312,316,320,324,328,332,336,340,344,348,352,356,36..., dimensions={0} | all-to-all | bytes 524288 | tf_op jit(solution)/shard_map/all_to_all | solution.py:163
  56.6 0.2 shard_map.94
  56.9 1.3 %collective-permute-start = (bf16[256,512]{1,0:T(8,128)(2,1)S(1)}, bf16[256,512]{1,0:T(8,128)(2,1)S(1)}, u32[]{:S(2)}, u32[]{:S(2)}) collective-permute-start(bf16[256,512]{1,0:T(8,128)(2,1)S(1)} %shard_map.94), channel_id=1, source_target_pairs={{1,0},{2,1},{3,2},{5,4},{6,5},{7,6},{9,8},{10,9},{11,10},{13,12},{... | collective-permute-start | bytes 786440 | tf_op jit(solution)/shard_map/ppermute | solution.py:242
  58.2 7.9 %collective-permute-done = bf16[256,512]{1,0:T(8,128)(2,1)S(1)} collective-permute-done((bf16[256,512]{1,0:T(8,128)(2,1)S(1)}, bf16[256,512]{1,0:T(8,128)(2,1)S(1)}, u32[]{:S(2)}, u32[]{:S(2)}) %collective-permute-start) | collective-permute-done | bytes 262176 | tf_op jit(solution)/shard_map/ppermute | solution.py:242
  66.0 0.7 %copy.11 = bf16[1,256,512]{2,1,0:T(8,128)(2,1)} copy(bf16[1,256,512]{2,1,0:T(8,128)(2,1)S(1)} %bitcast.7) | data formatting | bytes 524288
  (1 shorter events, 0.0 us)
Async XLA Ops:
  0.0 0.9 %copy-start = (bf16[1,256,512]{2,1,0:T(8,128)(2,1)S(1)}, bf16[1,256,512]{2,1,0:T(8,128)(2,1)}, u32[]{:S(2)}) copy-start(bf16[1,256,512]{2,1,0:T(8,128)(2,1)} %upper_ref.3) | copy-start | bytes 786436
  0.0 1.0 %copy-start.3 = (bf16[1,256,512]{2,1,0:T(8,128)(2,1)S(1)}, bf16[1,256,512]{2,1,0:T(8,128)(2,1)}, u32[]{:S(2)}) copy-start(bf16[1,256,512]{2,1,0:T(8,128)(2,1)} %w_out_ref.1) | copy-start | bytes 786436
  0.0 1.1 %copy-start.2 = (bf16[1,256,512]{2,1,0:T(8,128)(2,1)S(1)}, bf16[1,256,512]{2,1,0:T(8,128)(2,1)}, u32[]{:S(2)}) copy-start(bf16[1,256,512]{2,1,0:T(8,128)(2,1)} %rows_ref.1) | copy-start | bytes 786436
  0.0 1.1 %copy-start.7 = (s32[1,1,256]{2,1,0:T(1,128)S(1)}, s32[1,1,256]{2,1,0:T(1,128)}, u32[]{:S(2)}) copy-start(s32[1,1,256]{2,1,0:T(1,128)} %param.16) | copy-start | bytes 3076
  0.0 1.1 %copy-start.5 = (f32[1,512]{1,0:T(1,128)S(1)}, f32[1,512]{1,0:T(1,128)}, u32[]{:S(2)}) copy-start(f32[1,512]{1,0:T(1,128)} %shift_in.1) | copy-start | bytes 6148
  0.1 1.1 %copy-start.4 = (f32[1,512]{1,0:T(1,128)S(1)}, f32[1,512]{1,0:T(1,128)}, u32[]{:S(2)}) copy-start(f32[1,512]{1,0:T(1,128)} %gain_in.1) | copy-start | bytes 6148
  0.1 1.0 %copy-start.6 = (s32[1,1,256]{2,1,0:T(1,128)S(1)}, s32[1,1,256]{2,1,0:T(1,128)}, u32[]{:S(2)}) copy-start(s32[1,1,256]{2,1,0:T(1,128)} %param.15) | copy-start | bytes 3076
  0.1 1.0 %copy-start.8 = (s32[1,1,2]{2,1,0:T(1,128)S(1)}, s32[1,1,2]{2,1,0:T(1,128)}, u32[]{:S(2)}) copy-start(s32[1,1,2]{2,1,0:T(1,128)} %param.17) | copy-start | bytes 28
  1.1 31.1 %copy-start.1 = (bf16[1,512,768]{2,1,0:T(8,128)(2,1)S(1)}, bf16[1,512,768]{2,1,0:T(8,128)(2,1)}, u32[]{:S(2)}) copy-start(bf16[1,512,768]{2,1,0:T(8,128)(2,1)} %w_ref.1) | copy-start | bytes 2359300
  56.9 9.2 %collective-permute-start = (bf16[256,512]{1,0:T(8,128)(2,1)S(1)}, bf16[256,512]{1,0:T(8,128)(2,1)S(1)}, u32[]{:S(2)}, u32[]{:S(2)}) collective-permute-start(bf16[256,512]{1,0:T(8,128)(2,1)S(1)} %shard_map.94), channel_id=1, source_target_pairs={{1,0},{2,1},{3,2},{5,4},{6,5},{7,6},{9,8},{10,9},{11,10},{13,12},{... | collective-permute-start | bytes 786440 | tf_op jit(solution)/shard_map/ppermute | solution.py:242
